TPU v7x, 32 devices: a whole 2x2x4 slice. The times are simulated.
32 devices in a mesh: seq: 8 (over z, y), head: 4 (over x, core).
Axes of the slice: x: 2, y: 2, z: 4, core: 2. Of those that a mesh axis runs over, the one named last changes fastest.
Arguments:
- x_in: bfloat16 [4096, 8192], P('seq', 'head'), may hold values from -6 to 6
- bc_in: bfloat16 [4096, 4, 256], P('seq', 'head'), may hold values from -6 to 6
- z_in: bfloat16 [4096, 8192], P('seq', 'head'), may hold values from -6 to 6
- dt_raw: bfloat16 [128, 4096], P('head', 'seq'), may hold values from -20 to 4
- a_log: float32 [128], P('head'), may hold values from -6 to 0.7
- conv_x: float32 [4, 8192], P(None, 'head'), may hold values from -3 to 3
- conv_bc: float32 [4, 4, 256], P(None, 'head'), may hold values from -3 to 3
- d_skip: float32 [128], P('head'), may hold values from 0.5 to 2
- norm_gain: float32 [8192], P('head'), may hold values from 0.25 to 1.75
- out_weight: bfloat16 [8192, 4096], P('head'), may hold values from -0.09375 to 0.09375
Outputs:
- out: bfloat16 [4096, 4096], P('head', 'seq')
All inputs are finite; a program needn't handle non-finite values.
Results may differ from a plain program's by a relative error of at most 0.02.
Values may be sent and summed in bfloat16 or wider, within the bound.
A program may use at most 192 MiB of HBM per device.

v0:
```python
import jax
import jax.numpy as jnp
from jax import lax
from jax.sharding import PartitionSpec as P

SPAN = 128


def shifted(value, axis, steps):
    count = lax.axis_size(axis)
    leading, last = (max(0, -steps), min(count, count - steps))
    return lax.ppermute(value, axis, [(source, source + steps) for source in range(leading, last)])


def entering_2(shard, axis, join, neutral):
    place = lax.axis_index(axis)
    gathered = jax.tree.map(
        lambda a, kind: lax.all_gather(a.astype(kind), axis),
        shard,
        jax.tree.map(lambda a: jnp.bfloat16 if a.dtype == jnp.float32 else a.dtype, shard),
    )
    state = jax.tree.map(lambda a, e: jnp.zeros_like(a) + jnp.asarray(e, a.dtype), shard, neutral)

    def one(lap, state):
        return join(
            state,
            jax.tree.map(
                lambda a, own: lax.dynamic_index_in_dim(a, lap, 0, False).astype(own.dtype),
                gathered,
                shard,
            ),
        )

    return lax.fori_loop(0, place, one, state)


def conv_silu(extended, weight, rows):
    running = weight[0] * extended[0:rows].astype(jnp.float32)
    for offset in range(1, weight.shape[0]):
        running = running + weight[offset] * extended[offset : offset + rows].astype(jnp.float32)
    return (running * jax.nn.sigmoid(running)).astype(jnp.bfloat16)


def combine(earlier, later_pair):
    return (earlier[0] * later_pair[0], later_pair[0][:, None, None] * earlier[1] + later_pair[1])


def on_device(x_in, bc_in, z_in, dt_raw, a_log, conv_x, conv_bc, d_skip, norm_gain, out_weight):
    tok_rows, inner_dev = x_in.shape
    heads_dev = dt_raw.shape[0]
    groups_dev = bc_in.shape[1]
    state_size = bc_in.shape[2] // 2
    head_size = inner_dev // heads_dev
    per_group = heads_dev // groups_dev
    rim_rows = conv_x.shape[0] - 1
    blocks = tok_rows // SPAN
    prev_x, prev_bc = shifted((x_in[tok_rows - rim_rows :], bc_in[tok_rows - rim_rows :]), "seq", 1)
    x_conv = conv_silu(jnp.concatenate([prev_x, x_in], 0), conv_x, tok_rows)
    bc_conv = conv_silu(jnp.concatenate([prev_bc, bc_in], 0), conv_bc, tok_rows)
    b_blocks = bc_conv[:, :, :state_size].reshape(blocks, SPAN, groups_dev, state_size)
    c_blocks = bc_conv[:, :, state_size:].reshape(blocks, SPAN, groups_dev, state_size)
    x_blocks = x_conv.reshape(blocks, SPAN, groups_dev, per_group, head_size)
    step_size = jax.nn.softplus(dt_raw.astype(jnp.float32))
    rate = -jnp.exp(a_log)[:, None] * step_size
    step_blocks = jnp.transpose(
        step_size.reshape(groups_dev, per_group, blocks, SPAN), (2, 0, 1, 3)
    )
    rate_blocks = jnp.transpose(rate.reshape(groups_dev, per_group, blocks, SPAN), (2, 0, 1, 3))
    log_decay = jnp.cumsum(rate_blocks, axis=3)
    scores = jnp.einsum("ctgn,csgn->cgts", c_blocks, b_blocks, preferred_element_type=jnp.float32)
    row_ids = lax.broadcasted_iota(jnp.int32, (SPAN, SPAN), 0)
    col_ids = lax.broadcasted_iota(jnp.int32, (SPAN, SPAN), 1)
    causal = row_ids >= col_ids
    decay_gap = log_decay[..., :, None] - log_decay[..., None, :]
    mask_decay = jnp.where(causal, jnp.exp(jnp.where(causal, decay_gap, 0.0)), 0.0)
    mixing = (scores[:, :, None] * mask_decay * step_blocks[..., None, :]).astype(jnp.bfloat16)
    y_intra = jnp.einsum("cghts,csghp->ctghp", mixing, x_blocks, preferred_element_type=jnp.float32)
    tail_weight = jnp.exp(log_decay[..., -1:] - log_decay) * step_blocks
    b_heads = jnp.transpose(b_blocks, (0, 2, 1, 3))[:, :, None].astype(jnp.float32)
    weighted_b = (tail_weight[..., None] * b_heads).astype(jnp.bfloat16)
    block_states = jnp.einsum(
        "csghp,cghsn->cghpn", x_blocks, weighted_b, preferred_element_type=jnp.float32
    )
    block_decay = jnp.exp(log_decay[..., -1])

    def advance(running, inputs):
        running_state, running_decay = running
        decay_now, state_now = inputs
        updated = (
            decay_now[..., None, None] * running_state + state_now,
            running_decay * decay_now,
        )
        return (updated, (running_state, running_decay))

    start_pair = (
        jnp.zeros((groups_dev, per_group, head_size, state_size), jnp.float32),
        jnp.ones((groups_dev, per_group), jnp.float32),
    )
    (final_state, final_decay), (local_in, decay_in) = lax.scan(
        advance, start_pair, (block_decay, block_states)
    )
    own_pair = (
        final_decay.reshape(heads_dev),
        final_state.reshape(heads_dev, head_size, state_size),
    )
    identity = (
        jnp.ones((heads_dev,), jnp.float32),
        jnp.zeros((heads_dev, head_size, state_size), jnp.float32),
    )
    incoming = entering_2(own_pair, "seq", combine, identity)
    carried = incoming[1].reshape(groups_dev, per_group, head_size, state_size)
    entering = local_in + decay_in[..., None, None] * carried[None]
    readout = jnp.einsum(
        "ctgn,cghpn->cghtp", c_blocks.astype(jnp.float32), entering, precision=lax.Precision.HIGHEST
    )
    y_state = jnp.exp(log_decay)[..., None] * readout
    summed = (
        y_intra
        + jnp.transpose(y_state, (0, 3, 1, 2, 4))
        + d_skip.reshape(groups_dev, per_group, 1) * x_blocks.astype(jnp.float32)
    )
    gated_rows = summed.reshape(tok_rows, inner_dev) * jax.nn.silu(z_in.astype(jnp.float32))
    grouped = gated_rows.reshape(tok_rows, groups_dev, inner_dev // groups_dev)
    inverse_rms = lax.rsqrt(jnp.mean(grouped * grouped, axis=2, keepdims=True) + 1e-05)
    normed = ((grouped * inverse_rms).reshape(tok_rows, inner_dev) * norm_gain).astype(jnp.bfloat16)
    return lax.psum_scatter(
        lax.dot_general(
            out_weight, normed, (((0,), (1,)), ((), ())), preferred_element_type=jnp.float32
        ).astype(jnp.bfloat16),
        "head",
        scatter_dimension=0,
        tiled=True,
    )


def solution(mesh):
    placed = (
        P("seq", "head"),
        P("seq", "head", None),
        P("seq", "head"),
        P("head", "seq"),
        P("head"),
        P(None, "head"),
        P(None, "head", None),
        P("head"),
        P("head"),
        P("head", None),
    )
    return jax.shard_map(
        on_device, mesh=mesh, in_specs=placed, out_specs=P("head", "seq"), check_vma=False
    )
```

profile of v0, /device:TPU:24, one launch (start us, length us, event | category | flops | bytes accessed | tf_op | source)
XLA Modules:
  0.0 219.8 jit_solution(12580194864441463698)
XLA Ops:
  7.7 3.4 %collective-permute-start = (bf16[3,2048]{0,1:T(8,128)(2,1)S(1)}, bf16[3,2048]{0,1:T(8,128)(2,1)S(1)}, u32[]{:S(2)}, u32[]{:S(2)}) collective-permute-start(bf16[3,2048]{0,1:T(8,128)(2,1)S(1)} %copy.30), channel_id=1, source_target_pairs={{0,4},{4,8},{8,12},{12,16},{16,20},{20,24},{24,28},{1,5},{5,9},{9,... | collective-permute-start | bytes 36872 | tf_op jit(solution)/shard_map/ppermute | solution.py:12
  11.8 1.9 collective-permute-start.1
  13.7 1.5 fusion.43
  16.8 1.2 reduce_window_sum.11
  19.6 3.9 %copy.31 = bf16[512,2048]{0,1:T(8,128)(2,1)} copy(bf16[512,2048]{1,0:T(8,128)(2,1)} %param.14) | data formatting | bytes 4194304 | tf_op args[0]
  26.1 9.6 %multiply_convert_fusion.5 = bf16[512,2048]{0,1:T(8,128)(2,1)S(1)} fusion(bf16[512,2048]{0,1:T(8,128)(2,1)} %copy.31, bf16[3,2048]{0,1:T(8,128)(2,1)} %copy-done.3, f32[2048]{0:T(1024)} %bitcast.121, f32[2048]{0:T(1024)} %bitcast.122, f32[2048]{0:T(1024)} %bitcast.120, f32[2048]{0:T(1024)S(1)} %bitcast.119), kind=kLoop, calls=%fused_computation.38 | loop fusion | flops 26214400 | bytes 4239360 | tf_op jit(solution)/shard_map/convert_element_type | solution.py:41
  35.7 2.1 reshape.182
  37.8 5.3 %fusion.22 = f32[4,1,32,64,128]{4,3,2,1,0:T(8,128)} fusion(f32[4,128,128]{2,1,0:T(8,128)} %convert_element_type.118, f32[4,32,128]{2,1,0:T(8,128)} %fusion.39, bf16[4,128,32,64]{1,0,3,2:T(4,128)(2,1)} %reshape.182), kind=kOutput, calls=%fused_computation.44 | convolution fusion | flops 272629760 | bytes 6619136 | tf_op jit(solution)/shard_map/csghp,cghsn->cghpn/dot_general | solution.py:81
  43.1 10.1 %while.30 = (s32[]{:T(128)}, f32[1,32,64,128]{3,2,1,0:T(8,128)S(1)}, f32[1,32]{1,0:T(1,128)S(1)}, f32[4,1,32,64,128]{4,3,2,1,0:T(8,128)}, f32[4,1,32]{2,1,0:T(1,...) while((s32[]{:T(128)}, ...), condition=%wide.region_2.3_spmd.clone, body=%wide.region_1.2_spmd.clone.sunk | while | flops 1048675 | bytes 5245306 | solution.py:99
  44.2 1.4 bitcast_add_fusion.2
  46.7 1.4 bitcast_add_fusion.2
  49.3 1.4 bitcast_add_fusion.2
  50.7 1.1 bitcast_dynamic-update-slice_fusion.2
  51.8 1.4 bitcast_add_fusion.2
  54.8 3.9 %copy.41 = bf16[512,2048]{0,1:T(8,128)(2,1)} copy(bf16[512,2048]{1,0:T(8,128)(2,1)} %param.16) | data formatting | bytes 4194304 | tf_op args[2]
  60.3 3.1 %reshape.191 = f32[4,128,1,32,64]{1,0,4,3,2:T(4,128)} reshape(bf16[512,2048]{0,1:T(8,128)(2,1)S(1)} %multiply_convert_fusion.5) | data formatting | bytes 6291456 | tf_op jit(solution)/shard_map/convert_element_type | solution.py:120
  63.4 15.3 %all-gather = bf16[8,1,32]{2,1,0:T(2,128)(2,1)S(1)} all-gather(bf16[1,1,32]{2,1,0:T(2,128)(2,1)S(1)} %convert_bitcast_fusion), channel_id=1, replica_groups=mesh['seq'=8,'head'=4] {'seq'}, dimensions={0}, use_global_device_ids=true | all-gather | bytes 576 | tf_op jit(solution)/shard_map/all_gather | solution.py:18
  78.6 48.2 %all-gather.3.cloned.1.call-done = bf16[8,32,64,128]{3,2,1,0:T(8,128)(2,1)} async-done(((bf16[1,32,64,128]{3,2,1,0:T(8,128)(2,1)}), bf16[8,32,64,128]{3,2,1,0:T(8,128)(2,1)}) %all-gather.3.cloned.1.call-update) | async-done | bytes 4194320 | tf_op jit(solution)/shard_map/all_gather | solution.py:18
  127.0 8.3 %while.29 = (s32[]{:T(128)}, f32[32,64,128]{2,1,0:T(8,128)S(1)}, s32[]{:T(128)}, bf16[8,32]{1,0:T(8,128)(2,1)S(1)}, bf16[8,32,64,128]{3,2,1,0:T(8,128)(2,1)}, /*index=5*/s32[]{:T(128)}, s32[]{:T(128)}, s32[]{:T(128)}) while((s32[]{:T(128)}, f32[32,64,128]{2,1,0:T(8,128)S(1)}, s32[]{:T(128)}, bf16[8,32]{1,0:T(8,128)(2,1)S(1)}, ...), condition=%wide.region_4.5_spmd, body=%wide.region_3.4_spmd.sunk | while | flops 786469 | bytes 2621887 | solution.py:34
  127.0 1.3 convert_add_fusion.2
  128.4 1.3 convert_add_fusion.2
  129.7 1.3 convert_add_fusion.2
  131.1 1.3 convert_add_fusion.2
  132.4 1.3 convert_add_fusion.2
  133.8 1.3 convert_add_fusion.2
  135.4 4.8 %fusion.10 = f32[4,32,64,128]{3,2,1,0:T(8,128)S(1)} fusion(bf16[4,128,128,1]{2,1,3,0:T(8,128)(2,1)S(1)} %bitcast.115, f32[4,1,32,64,128]{4,3,2,1,0:T(8,128)} %get-tuple-element.89, f32[32,64,128]{2,1,0:T(8,128)S(1)} %get-tuple-element.93, f32[4,32]{1,0:T(4,128)S(1)} %bitcast.129), kind=kOutput, calls=%fused_computation.24 | convolution fusion | flops 1612709888 | bytes 9568768 | tf_op jit(solution)/shard_map/ctgn,cghpn->cghtp/dot_general | solution.py:113
  140.2 3.8 %fusion.9 = f32[4,128,1,32,64]{1,4,3,0,2:T(8,128)S(1)} fusion(f32[4,32,64,128]{3,2,1,0:T(8,128)S(1)} %fusion.10, f32[4,128,1,32,64]{1,0,4,3,2:T(4,128)S(1)} %copy-done.1, f32[32]{0:T(128)S(1)} %copy-done.10, f32[4,128,32]{1,2,0:T(8,128)S(1)} %exponential_bitcast_fusion, f32[4,32,128]{2,1,0:T(8,128)S(1)} %bitcast.118, f32[4,32,128]{2,1,0:T(8,128)S(1)} %bitcast.116, ...), kind=kOutput, calls=%fused_computation.23 | convolution fusion | flops 285212672 | bytes 15155328 | tf_op jit(solution)/shard_map/cghts,csghp->ctghp/dot_general | solution.py:77
  144.0 3.6 %copy.40 = f32[4,128,1,32,64]{1,0,4,3,2:T(4,128)S(1)} copy(f32[4,128,1,32,64]{1,4,3,0,2:T(8,128)S(1)} %fusion.9) | data formatting | bytes 8388608 | tf_op jit(solution)/shard_map/add | solution.py:118
  147.7 1.4 multiply_reduce_fusion
  149.1 15.5 %fusion.1 = bf16[4096,512]{0,1:T(8,128)(2,1)} fusion(bf16[2048,4096]{1,0:T(8,128)(2,1)} %param.23, f32[2048]{0:T(1024)S(1)} %copy-done.9, f32[512]{0:T(512)S(1)} %add_rsqrt_fusion, bf16[512,2048]{0,1:T(8,128)(2,1)S(1)} %copy-done, f32[256,8,4,128]{3,2,1,0:T(4,128)S(1)} %bitcast.111), kind=kOutput, calls=%fused_computation.12 | convolution fusion | flops 8601468928 | bytes 27273216 | tf_op jit(solution)/shard_map/dot_general | solution.py:127
  164.7 46.0 %reduce-scatter.2.cloned.1.call-done = bf16[1024,512]{0,1:T(8,128)(2,1)} async-done(((bf16[4096,512]{0,1:T(8,128)(2,1)}), bf16[1024,512]{0,1:T(8,128)(2,1)}) %reduce-scatter.2.cloned.1.call-update) | async-done | bytes 1048592 | tf_op jit(solution)/shard_map/reduce_scatter | solution.py:126
  210.7 2.3 %copy.42 = bf16[1024,512]{1,0:T(8,128)(2,1)} copy(bf16[1024,512]{0,1:T(8,128)(2,1)} %reduce-scatter.2.cloned.1.call-done) | data formatting | bytes 2097152 | tf_op jit(solution)/shard_map/reduce_scatter | solution.py:126
  (76 shorter events, 14.2 us)
Async XLA Ops:
  6.5 17.6 %copy-start.4 = (bf16[512,1,256]{2,0,1:T(8,128)(2,1)S(1)}, bf16[512,1,256]{2,0,1:T(8,128)(2,1)}, u32[]{:S(2)}) copy-start(bf16[512,1,256]{2,0,1:T(8,128)(2,1)} %param.15) | copy-start | bytes 786436
  6.5 120.3 %all-gather.3.cloned.1.call-start = ((), (), s32[]{:S(2)}) async-start(), calls=%async_computation.1 | async-start | bytes 4718592 | tf_op jit(solution)/shard_map/all_gather | solution.py:18
  7.7 17.6 %collective-permute-start = (bf16[3,2048]{0,1:T(8,128)(2,1)S(1)}, bf16[3,2048]{0,1:T(8,128)(2,1)S(1)}, u32[]{:S(2)}, u32[]{:S(2)}) collective-permute-start(bf16[3,2048]{0,1:T(8,128)(2,1)S(1)} %copy.30), channel_id=1, source_target_pairs={{0,4},{4,8},{8,12},{12,16},{16,20},{20,24},{24,28},{1,5},{5,9},{9,... | collective-permute-start | bytes 36872 | tf_op jit(solution)/shard_map/ppermute | solution.py:12
  11.8 12.4 %collective-permute-start.1 = (bf16[3,1,256]{2,0,1:T(4,128)(2,1)S(1)}, bf16[3,1,256]{2,0,1:T(4,128)(2,1)S(1)}, u32[]{:S(2)}, u32[]{:S(2)}) collective-permute-start(bf16[3,1,256]{2,0,1:T(4,128)(2,1)S(1)} %slice.67), channel_id=1, source_target_pairs={{0,4},{4,8},{8,12},{12,16},{16,20},{20,24},{24,28},{1,5},{5,9},{9,... | collective-permute-start | bytes 4616 | tf_op jit(solution)/shard_map/ppermute | solution.py:12
  25.3 0.8 copy-start.3
  37.8 5.3 %copy-start.8 = (f32[4,1,32]{2,1,0:T(1,128)S(1)}, f32[4,1,32]{2,1,0:T(1,128)}, u32[]{:S(2)}) copy-start(f32[4,1,32]{2,1,0:T(1,128)} %custom-call.3) | copy-start | bytes 1540
  54.2 156.5 %reduce-scatter.2.cloned.1.call-start = ((), (), s32[]{:S(2)}) async-start(), calls=%async_computation.2 | async-start | bytes 5242880 | tf_op jit(solution)/shard_map/reduce_scatter | solution.py:126
  135.3 4.9 %copy-start.1 = (f32[4,128,1,32,64]{1,0,4,3,2:T(4,128)S(1)}, f32[4,128,1,32,64]{1,0,4,3,2:T(4,128)}, u32[]{:S(2)}) copy-start(f32[4,128,1,32,64]{1,0,4,3,2:T(4,128)} %reshape.191) | copy-start | bytes 12582916
  135.3 4.9 %copy-start.2 = (bf16[4,128,32,64]{1,0,3,2:T(4,128)(2,1)S(1)}, bf16[4,128,32,64]{1,0,3,2:T(4,128)(2,1)}, u32[]{:S(2)}) copy-start(bf16[4,128,32,64]{1,0,3,2:T(4,128)(2,1)} %reshape.182) | copy-start | bytes 6291460
  135.3 4.9 %copy-start.5 = (f32[4,128,128]{2,1,0:T(8,128)S(1)}, f32[4,128,128]{2,1,0:T(8,128)}, u32[]{:S(2)}) copy-start(f32[4,128,128]{2,1,0:T(8,128)} %fusion.45) | copy-start | bytes 786436
  135.3 4.9 %copy-start.6 = (f32[1,32,4,128]{3,1,0,2:T(8,128)S(1)}, f32[1,32,4,128]{3,1,0,2:T(8,128)}, u32[]{:S(2)}) copy-start(f32[1,32,4,128]{3,1,0,2:T(8,128)} %copy.66) | copy-start | bytes 196612
  135.3 4.9 %copy-start.7 = (pred[128,128]{1,0:T(8,128)(4,1)S(1)}, pred[128,128]{1,0:T(8,128)(4,1)}, u32[]{:S(2)}) copy-start(pred[128,128]{1,0:T(8,128)(4,1)} %iota_compare_fusion) | copy-start | bytes 49156
  135.3 4.9 %copy-start.10 = (f32[32]{0:T(128)S(1)}, f32[32]{0:T(128)}, u32[]{:S(2)}) copy-start(f32[32]{0:T(128)} %param.21) | copy-start | bytes 388
  144.0 3.6 %copy-start = (bf16[512,2048]{0,1:T(8,128)(2,1)S(1)}, bf16[512,2048]{0,1:T(8,128)(2,1)}, u32[]{:S(2)}) copy-start(bf16[512,2048]{0,1:T(8,128)(2,1)} %copy.41) | copy-start | bytes 6291460
  147.6 1.5 copy-start.9
Sparse Core Ops, SparseCore 0:
  54.3 72.5 all-gather.2
  164.8 45.8 reduce-scatter.1
where the time goes:
time: 223 us; the launch traced here: 220 us
  waiting for transfers between devices  94.9 us (43%)
  other arithmetic  34.9 us (16%)
  matrix products  30.3 us (14%)
  local copies, waits for them, and re-layouts  24.8 us (11%)
  blocking collectives  15.3 us (7%)
  between operations  13.7 us (6%)
  starting transfers between devices  5.38 us (2%)
    all_gather x1, waiting for transfers between devices, entering_2(): lax.all_gather(a.astype(kind), axis)  48.2 us
    reduce_scatter x1, waiting for transfers between devices, on_device(): lax.psum_scatter(lax.dot_general(out_weight, normed, (((0,), (1,)), ((),...  46 us
    dot_general x1, matrix products, on_device(): lax.dot_general(out_weight, normed, (((0,), (1,)), ((), ())), preferred_e...  15.5 us
    all_gather x1, blocking collectives, entering_2(): lax.all_gather(a.astype(kind), axis)  15.3 us
    convert_element_type x2, other arithmetic, conv_silu(): return (running * jax.nn.sigmoid(running)).astype(jnp.bfloat16)  9.97 us
    unnamed x25, local copies, waits for them, and re-layouts  8.68 us
    add x6, other arithmetic, combine(): later_pair[0][:, None, None] * earlier[1] + later_pair[1]  7.81 us
    add x4, other arithmetic, advance(): decay_now[..., None, None] * running_state + state_now  5.62 us
  transfers between devices with their start and end apart: 4, of which 3 were waited for; matrix products, arithmetic and copies ran while one was open for 9% of the time, Pallas kernels for 0%

commit v1 on v0

v1 whole, which is shorter than its diff:
```python
import functools

import jax
import jax.numpy as jnp
from jax import lax
from jax.experimental import pallas as pl
from jax.experimental.pallas import tpu as pltpu
from jax.sharding import PartitionSpec as P

SPAN = 128
MESH = pl.DeviceIdType.MESH
F32 = jnp.float32
BF16 = jnp.bfloat16
LANES = 512
RIM = 16


def half_tanh_silu(u):
    return 0.5 * u * (1.0 + jnp.tanh(0.5 * u))


def conv_silu(before, now, taps):
    cat = jnp.concatenate([before.astype(F32), now.astype(F32)], 0)
    width = taps.shape[0]
    total = taps[width - 1 : width] * cat[RIM:]
    for k in range(width - 1):
        total = total + taps[k : k + 1] * pltpu.roll(cat, width - 1 - k, 0)[RIM:]
    return half_tanh_silu(total)


def split_two(value):
    high = value.astype(BF16)
    low = (value - high.astype(F32)).astype(BF16)
    return jnp.concatenate([high, low], 1)


def scan_kernel(
    n_seq, x_ref, bc_ref, z_ref, dt_ref, alog_ref, cx_ref, cbc_ref, skip_ref, gain_ref, out_ref,
    halo_x, halo_bc, xconv, b_t, c_mat, score, ld_row, st_row, ld_col, t_split, pick_tail, pick_exp,
    decay_in, decay_blk, decay_own, decay_other, skip_row, local_in, final, y_ref, enter,
    y_send, y_recv, z_send, z_recv,
    halo_sems, dec_sems, ys_sem, yr_sem, zs_sem, zr_sem,
):
    tokens, inner = x_ref.shape
    heads = dt_ref.shape[0]
    state = b_t.shape[1]
    width = inner // heads
    blocks = tokens // SPAN
    chunks = inner // LANES
    per = heads // chunks
    rows = n_seq // 2
    q = lax.axis_index("seq")
    odd = lax.rem(q, 2)
    place = q // 2
    pair = q + 1 - 2 * odd
    after = lax.rem(q + 1, n_seq)
    ahead = lax.rem(q + 2, n_seq)

    barrier = pltpu.get_barrier_semaphore()
    pl.semaphore_signal(barrier, inc=1, device_id={"seq": pair}, device_id_type=MESH)

    @pl.when(q > 0)
    def _():
        pl.semaphore_signal(barrier, inc=1, device_id={"seq": q - 1}, device_id_type=MESH)

    @pl.when(q > 1)
    def _():
        pl.semaphore_signal(barrier, inc=1, device_id={"seq": q - 2}, device_id_type=MESH)

    peers = 1 + jnp.minimum(n_seq - 1 - q, 1) + jnp.minimum(jnp.maximum(n_seq - 2 - q, 0), 1)
    pl.semaphore_wait(barrier, peers)

    def send(src, dst, s, r, to):
        return pltpu.make_async_remote_copy(
            src_ref=src, dst_ref=dst, send_sem=s, recv_sem=r, device_id={"seq": to}, device_id_type=MESH
        )

    halo_copies = [
        send(x_ref.at[pl.ds(tokens - RIM, RIM)], halo_x, halo_sems.at[0], halo_sems.at[1], after),
        send(bc_ref.at[pl.ds(tokens - RIM, RIM)], halo_bc, halo_sems.at[2], halo_sems.at[3], after),
    ]

    @pl.when(q < n_seq - 1)
    def _():
        for copy in halo_copies:
            copy.start()

    r_id = lax.broadcasted_iota(jnp.int32, (SPAN, SPAN), 0)
    c_id = lax.broadcasted_iota(jnp.int32, (SPAN, SPAN), 1)
    upto = jnp.where(r_id <= c_id, 1.0, 0.0).astype(F32)
    hr = lax.broadcasted_iota(jnp.int32, (heads, heads), 0)
    hc = lax.broadcasted_iota(jnp.int32, (heads, heads), 1)
    neg_a = -jnp.sum(jnp.where(hr == hc, jnp.exp(alog_ref[...]), 0.0), axis=1, keepdims=True)
    p_row = lax.rem(lax.broadcasted_iota(jnp.int32, (2 * SPAN, inner), 0), SPAN)
    p_head = lax.broadcasted_iota(jnp.int32, (2 * SPAN, inner), 1) // width
    pick_tail[...] = jnp.where(p_row == heads + p_head, 1.0, 0.0).astype(BF16)
    pick_exp[...] = jnp.where(p_row == 2 * heads + p_head, 1.0, 0.0).astype(BF16)
    skip_pad = jnp.concatenate(
        [jnp.zeros((8, 2 * heads), F32), jnp.broadcast_to(skip_ref[...], (8, heads)), jnp.zeros((8, heads), F32)], 1
    )
    skip_row[...] = jnp.dot(split_two(skip_pad), pick_exp[...], preferred_element_type=F32)
    running = jnp.ones((8, inner), F32)
    for b in range(blocks):
        dt = dt_ref[:, b * SPAN : (b + 1) * SPAN].astype(F32)
        e = jnp.exp(-jnp.abs(dt))
        log1p = jnp.where(e < 0.01, e * (1.0 - e * (0.5 - e * (1.0 / 3.0 - 0.25 * e))), jnp.log(1.0 + e))
        step = jnp.maximum(dt, 0.0) + log1p
        ld = jnp.dot(neg_a * step, upto, preferred_element_type=F32, precision=lax.Precision.HIGHEST)
        tail = jnp.exp(ld[:, SPAN - 1 : SPAN] - ld) * step
        table = jnp.concatenate([ld, tail, jnp.exp(ld), step], 0)
        if 4 * heads < SPAN:
            table = jnp.concatenate([table, jnp.zeros((SPAN - 4 * heads, SPAN), F32)], 0)
        turned = table.T
        ld_row[b] = ld
        st_row[b] = step
        for c in range(chunks):
            ld_col[b, c] = turned[:, c * per : (c + 1) * per]
        both = split_two(turned)
        t_split[b] = both
        last = jnp.dot(both[SPAN - 16 :], pick_exp[...], preferred_element_type=F32)[15:16]
        decay_in[b] = running
        decay_blk[b] = jnp.broadcast_to(last, (8, inner))
        running = running * last
    decay_own[...] = running
    dec_copy = send(decay_own, decay_other, dec_sems.at[0], dec_sems.at[1], pair)
    dec_copy.start()

    @pl.when(q > 0)
    def _():
        for copy in halo_copies:
            copy.wait_recv()

    @pl.when(q == 0)
    def _():
        halo_x[...] = jnp.zeros_like(halo_x)
        halo_bc[...] = jnp.zeros_like(halo_bc)

    for b in range(blocks):
        before = halo_bc[...] if b == 0 else bc_ref[b * SPAN - RIM : b * SPAN]
        bc = conv_silu(before, bc_ref[b * SPAN : (b + 1) * SPAN], cbc_ref[...])
        b_f = bc[:, :state].astype(BF16)
        c_f = bc[:, state:].astype(BF16)
        b_t[b] = bc[:, :state].T.astype(BF16)
        c_mat[b] = c_f
        sc = lax.dot_general(c_f, b_f, (((1,), (1,)), ((), ())), preferred_element_type=F32)
        score[b] = jnp.where(r_id >= c_id, sc, 0.0)

    def y_copy(c):
        return send(y_send.at[c], y_recv.at[c], ys_sem.at[c], yr_sem.at[c], pair)

    def z_copy(c):
        return send(z_send.at[c], z_recv.at[c], zs_sem.at[c], zr_sem.at[c], ahead)

    def state_chunk(c, carry):
        lanes = pl.ds(pl.multiple_of(c * LANES, LANES), LANES)
        held = jnp.zeros((state, LANES), F32)
        for b in range(blocks):
            before = halo_x[:, lanes] if b == 0 else x_ref[pl.ds(b * SPAN - RIM, RIM), lanes]
            xc = conv_silu(before, x_ref[pl.ds(b * SPAN, SPAN), lanes], cx_ref[:, lanes]).astype(BF16)
            xconv[pl.ds(b * SPAN, SPAN), lanes] = xc
            tail = jnp.dot(t_split[b], pick_tail[:, lanes], preferred_element_type=F32)
            weighted = (xc.astype(F32) * tail).astype(BF16)
            local_in[b, :, lanes] = held
            new = jnp.dot(b_t[b], weighted, preferred_element_type=F32)
            held = decay_blk[b, 0:1, lanes] * held + new
        final[:, lanes] = held
        y_send[c] = held.astype(BF16)
        y_copy(c).start()
        return carry

    lax.fori_loop(0, chunks, state_chunk, 0)
    dec_copy.wait_recv()
    is_odd = odd.astype(F32)

    def serve(c):
        lanes = pl.ds(pl.multiple_of(c * LANES, LANES), LANES)
        y_copy(c).wait_recv()
        own = final[:, lanes]
        other = y_recv[c].astype(F32)
        d_own = decay_own[0:1, lanes]
        d_other = decay_other[0:1, lanes]
        enter[:, lanes] = is_odd * other

        @pl.when(place > 0)
        def _():
            z_copy(c).wait_recv()
            enter[:, lanes] += z_recv[c].astype(F32) * (1.0 - is_odd + is_odd * d_other)

        @pl.when(place < rows - 1)
        def _():
            both = own * (is_odd + (1.0 - is_odd) * d_other) + other * (1.0 - is_odd + is_odd * d_own)
            final[:, lanes] = both

            @pl.when(place > 0)
            def _():
                final[:, lanes] += d_own * d_other * z_recv[c].astype(F32)

            z_send[c] = final[:, lanes].astype(BF16)
            z_copy(c).start()

    half = lax.broadcasted_iota(jnp.int32, (1, 2 * width), 1) < width
    left = jnp.where(half, 1.0, 0.0).astype(BF16)
    right = jnp.where(half, 0.0, 1.0).astype(BF16)

    def intra(c):
        def one(b, carry):
            token = pl.ds(pl.multiple_of(b * SPAN, SPAN), SPAN)
            head = pl.ds(pl.multiple_of(c * per, per), per)
            lds = ld_row[b, head, :]
            sts = st_row[b, head, :]
            cols = ld_col[b, c]
            sc = score[b]
            for j in range(per // 2):
                lanes = pl.ds(pl.multiple_of(c * LANES + j * 2 * width, 2 * width), 2 * width)
                mixes = []
                for h in (2 * j, 2 * j + 1):
                    gap = jnp.minimum(cols[:, h : h + 1] - lds[h : h + 1], 0.0)
                    mixes.append((sc * jnp.exp(gap) * sts[h : h + 1]).astype(BF16))
                xc = xconv[token, lanes]
                y_ref[token, lanes] = jnp.dot(
                    jnp.concatenate(mixes, 1),
                    jnp.concatenate([xc * left, xc * right], 0),
                    preferred_element_type=F32,
                )
            return carry

        lax.fori_loop(0, blocks, one, 0)

    def slot(j, carry):
        c = j - place

        @pl.when((c >= 0) & (c < chunks))
        def _():
            serve(c)

        @pl.when(j < chunks)
        def _():
            intra(j)

        return carry

    lax.fori_loop(0, chunks + rows - 1, slot, 0)

    def finish(b, carry):
        token = pl.ds(pl.multiple_of(b * SPAN, SPAN), SPAN)
        power = jnp.zeros((SPAN, 1), F32)
        for c in range(chunks):
            lanes = pl.ds(c * LANES, LANES)
            grown = jnp.dot(t_split[b], pick_exp[:, lanes], preferred_element_type=F32)
            ent = (local_in[b, :, lanes] + decay_in[b, 0:1, lanes] * enter[:, lanes]).astype(BF16)
            read = jnp.dot(c_mat[b], ent, preferred_element_type=F32)
            total = y_ref[token, lanes] + grown * read + skip_row[0:1, lanes] * xconv[token, lanes].astype(F32)
            gated = total * half_tanh_silu(z_ref[token, lanes].astype(F32))
            y_ref[token, lanes] = gated
            power = power + jnp.sum(gated * gated, axis=1, keepdims=True)
        scale = lax.rsqrt(power * (1.0 / inner) + 1e-05)
        for c in range(chunks):
            lanes = pl.ds(c * LANES, LANES)
            out_ref[token, lanes] = (y_ref[token, lanes] * scale * gain_ref[:, lanes]).astype(BF16)
        return carry

    lax.fori_loop(0, blocks, finish, 0)

    dec_copy.wait_send()

    @pl.when(q < n_seq - 1)
    def _():
        for copy in halo_copies:
            copy.wait_send()

    def drain(c, carry):
        y_copy(c).wait_send()

        @pl.when(place < rows - 1)
        def _():
            z_copy(c).wait_send()

        return carry

    lax.fori_loop(0, chunks, drain, 0)


def project_kernel(
    n_ref, w_ref, out_ref, w_buf, s1, r1, s2, r2, s3, r3, keep,
    w_sem, s1s, s1r, s2s, s2r, s3s, s3r,
):
    h = lax.axis_index("head")
    core = lax.rem(h, 2)
    side = h // 2
    near = 2 * side + 1 - core
    far = 2 * (1 - side) + core
    cross = 3 - h
    pieces, cols = w_buf.shape[0] // 4, w_buf.shape[2]

    def fetch(block, c, slot):
        start = pl.multiple_of((block * pieces + c) * cols, cols)
        return pltpu.make_async_copy(w_ref.at[:, pl.ds(start, cols)], w_buf.at[slot], w_sem.at[slot])

    def fetch_first(c, carry):
        fetch(cross, c, 2 * c).start()
        fetch(far, c, 2 * c + 1).start()
        return carry

    def fetch_second(c, carry):
        fetch(near, c, 2 * pieces + 2 * c).start()
        fetch(h, c, 2 * pieces + 2 * c + 1).start()
        return carry

    lax.fori_loop(0, pieces, fetch_first, 0)
    lax.fori_loop(0, pieces, fetch_second, 0)

    barrier = pltpu.get_barrier_semaphore()
    for other in (near, far):
        pl.semaphore_signal(barrier, inc=1, device_id={"head": other}, device_id_type=MESH)
    pl.semaphore_wait(barrier, 2)

    def send(src, dst, s, r, to, c):
        return pltpu.make_async_remote_copy(
            src_ref=src.at[c], dst_ref=dst.at[c], send_sem=s.at[c], recv_sem=r.at[c],
            device_id={"head": to}, device_id_type=MESH,
        )

    def tile(block, c, slot):
        fetch(block, c, slot).wait()
        return jnp.dot(n_ref[...], w_buf[slot], preferred_element_type=F32)

    def first(c, carry):
        s1[c] = tile(cross, c, 2 * c).astype(BF16)
        send(s1, r1, s1s, s1r, near, c).start()
        keep[c] = tile(far, c, 2 * c + 1)
        send(s1, r1, s1s, s1r, near, c).wait_recv()
        s2[c] = (keep[c] + r1[c].astype(F32)).astype(BF16)
        send(s2, r2, s2s, s2r, far, c).start()
        return carry

    def second(c, carry):
        s3[c] = tile(near, c, 2 * pieces + 2 * c).astype(BF16)
        send(s3, r3, s3s, s3r, near, c).start()
        keep[c] = tile(h, c, 2 * pieces + 2 * c + 1)
        return carry

    def third(c, carry):
        send(s3, r3, s3s, s3r, near, c).wait_recv()
        send(s2, r2, s2s, s2r, far, c).wait_recv()
        total = keep[c] + r3[c].astype(F32) + r2[c].astype(F32)
        out_ref[pl.ds(pl.multiple_of(c * cols, cols), cols), :] = total.T.astype(BF16)
        return carry

    def drain(c, carry):
        send(s1, r1, s1s, s1r, near, c).wait_send()
        send(s2, r2, s2s, s2r, far, c).wait_send()
        send(s3, r3, s3s, s3r, near, c).wait_send()
        return carry

    lax.fori_loop(0, pieces, first, 0)
    lax.fori_loop(0, pieces, second, 0)
    lax.fori_loop(0, pieces, third, 0)
    lax.fori_loop(0, pieces, drain, 0)


def on_device(n_seq, x_in, bc_in, z_in, dt_raw, a_log, conv_x, conv_bc, d_skip, norm_gain, out_weight):
    tokens, inner = x_in.shape
    heads = dt_raw.shape[0]
    features = out_weight.shape[1]
    state = bc_in.shape[2] // 2
    blocks = tokens // SPAN
    chunks = inner // LANES
    per = heads // chunks
    vmem = pl.BlockSpec(memory_space=pltpu.VMEM)
    dma = pltpu.SemaphoreType.DMA
    normed = pl.pallas_call(
        functools.partial(scan_kernel, n_seq),
        name="scan",
        out_shape=jax.ShapeDtypeStruct((tokens, inner), BF16),
        in_specs=[vmem] * 9,
        out_specs=vmem,
        scratch_shapes=[
            pltpu.VMEM((RIM, inner), BF16),
            pltpu.VMEM((RIM, 2 * state), BF16),
            pltpu.VMEM((tokens, inner), BF16),
            pltpu.VMEM((blocks, state, SPAN), BF16),
            pltpu.VMEM((blocks, SPAN, state), BF16),
            pltpu.VMEM((blocks, SPAN, SPAN), F32),
            pltpu.VMEM((blocks, heads, SPAN), F32),
            pltpu.VMEM((blocks, heads, SPAN), F32),
            pltpu.VMEM((blocks, chunks, SPAN, per), F32),
            pltpu.VMEM((blocks, SPAN, 2 * SPAN), BF16),
            pltpu.VMEM((2 * SPAN, inner), BF16),
            pltpu.VMEM((2 * SPAN, inner), BF16),
            pltpu.VMEM((blocks, 8, inner), F32),
            pltpu.VMEM((blocks, 8, inner), F32),
            pltpu.VMEM((8, inner), F32),
            pltpu.VMEM((8, inner), F32),
            pltpu.VMEM((8, inner), F32),
            pltpu.VMEM((blocks, state, inner), F32),
            pltpu.VMEM((state, inner), F32),
            pltpu.VMEM((tokens, inner), F32),
            pltpu.VMEM((state, inner), F32),
            pltpu.VMEM((chunks, state, LANES), BF16),
            pltpu.VMEM((chunks, state, LANES), BF16),
            pltpu.VMEM((chunks, state, LANES), BF16),
            pltpu.VMEM((chunks, state, LANES), BF16),
            dma((4,)),
            dma((2,)),
            dma((chunks,)),
            dma((chunks,)),
            dma((chunks,)),
            dma((chunks,)),
        ],
        compiler_params=pltpu.CompilerParams(
            collective_id=0, has_side_effects=True, vmem_limit_bytes=48 * 2**20
        ),
    )(
        x_in,
        bc_in.reshape(tokens, 2 * state),
        z_in,
        dt_raw,
        a_log.reshape(1, heads),
        conv_x,
        conv_bc.reshape(conv_bc.shape[0], 2 * state),
        d_skip.reshape(1, heads),
        norm_gain.reshape(1, inner),
    )
    share = features // 4
    cols = min(256, share)
    pieces = share // cols
    part = pltpu.VMEM((pieces, tokens, cols), BF16)
    return pl.pallas_call(
        project_kernel,
        name="project",
        out_shape=jax.ShapeDtypeStruct((share, tokens), BF16),
        in_specs=[vmem, pl.BlockSpec(memory_space=pl.ANY)],
        out_specs=vmem,
        scratch_shapes=[pltpu.VMEM((4 * pieces, inner, cols), BF16)]
        + [part] * 6
        + [pltpu.VMEM((pieces, tokens, cols), F32), dma((4 * pieces,))]
        + [dma((pieces,))] * 6,
        compiler_params=pltpu.CompilerParams(
            collective_id=1, has_side_effects=True, vmem_limit_bytes=48 * 2**20
        ),
    )(normed, out_weight)


def solution(mesh):
    placed = (
        P("seq", "head"),
        P("seq", "head", None),
        P("seq", "head"),
        P("head", "seq"),
        P("head"),
        P(None, "head"),
        P(None, "head", None),
        P("head"),
        P("head"),
        P("head", None),
    )
    return jax.shard_map(
        functools.partial(on_device, mesh.shape["seq"]),
        mesh=mesh, in_specs=placed, out_specs=P("head", "seq"), check_vma=False,
    )
```

time: 223 us -> 73.9 us (0.33); the launches traced: 220 us -> 73.5 us
  waiting for transfers between devices: 94.9 us -> 0 us
  Pallas kernels: 0 us -> 65.7 us
  other arithmetic: 34.9 us -> 0 us
  matrix products: 30.3 us -> 0 us
  local copies, waits for them, and re-layouts: 24.8 us -> 7.72 us
  blocking collectives: 15.3 us -> 0 us
  between operations: 13.7 us -> 0.02 us
  starting transfers between devices: 5.38 us -> 0 us
    pallas_call x0 -> x2, Pallas kernels: none -> 65.7 us  [the longest x1 36.3 us: on_device(): pl.pallas_call(functools.partial(scan_kernel, n_seq), name='scan', out_sh...]
    all_gather x1 -> x0, waiting for transfers between devices: 48.2 us -> none  [entering_2(): lax.all_gather(a.astype(kind), axis)]
    reduce_scatter x1 -> x0, waiting for transfers between devices: 46 us -> none  [on_device(): lax.psum_scatter(lax.dot_general(out_weight, normed, (((0,), (1,)), ((),...]
    dot_general x5 -> x0, matrix products: 30.3 us -> none  [the longest x1 15.5 us: on_device(): lax.dot_general(out_weight, normed, (((0,), (1,)), ((), ())), preferred_e...]
    all_gather x1 -> x0, blocking collectives: 15.3 us -> none  [entering_2(): lax.all_gather(a.astype(kind), axis)]
    add x10 -> x0, other arithmetic: 13.4 us -> none  [the longest x6 7.81 us: combine(): later_pair[0][:, None, None] * earlier[1] + later_pair[1]]
    convert_element_type x10 -> x0, other arithmetic: 11.7 us -> none  [the longest x2 9.97 us: conv_silu(): return (running * jax.nn.sigmoid(running)).astype(jnp.bfloat16)]
    ppermute x2 -> x0, starting transfers between devices: 5.34 us -> none  [shifted(): lax.ppermute(value, axis, [(source, source + steps) for source in range(l...]
  transfers between devices with their start and end apart: 4 -> 0, of which waited for: 3 -> 0; matrix products, arithmetic and copies ran while one was open for 9% -> 0% of each run, Pallas kernels for 0% -> 0%
where the time goes in v1:
time: 73.9 us; the launch traced here: 73.5 us
  Pallas kernels  65.7 us (89%)
  local copies, waits for them, and re-layouts  7.72 us (10%)
    pallas_call x1, Pallas kernels, on_device(): pl.pallas_call(functools.partial(scan_kernel, n_seq), name='scan', out_sh...  36.3 us
    pallas_call x1, Pallas kernels, on_device(): pl.pallas_call(project_kernel, name='project', out_shape=jax.ShapeDtypeSt...  29.4 us
    unnamed x16, local copies, waits for them, and re-layouts  7.72 us

profile of v1, /device:TPU:24, one launch (start us, length us, event | category | flops | bytes accessed | tf_op | source)
XLA Modules:
  0.0 73.5 jit_solution(7631506772100641052)
XLA Ops:
  0.0 0.7 copy.13
  0.7 0.0 copy-start
  0.7 1.6 %copy-done = bf16[512,2048]{1,0:T(8,128)(2,1)S(1)} copy-done((bf16[512,2048]{1,0:T(8,128)(2,1)S(1)}, bf16[512,2048]{1,0:T(8,128)(2,1)}, u32[]{:S(2)}) %copy-start) | copy-done | bytes 2097176
  2.3 0.0 copy-start.1
  2.3 0.9 %copy-done.1 = bf16[512,1,256]{2,0,1:T(8,128)(2,1)S(1)} copy-done((bf16[512,1,256]{2,0,1:T(8,128)(2,1)S(1)}, bf16[512,1,256]{2,0,1:T(8,128)(2,1)}, u32[]{:S(2)}) %copy-start.1) | copy-done | bytes 262168
  3.2 0.0 copy-start.2
  3.2 0.8 %copy-done.2 = bf16[32,512]{1,0:T(8,128)(2,1)S(1)} copy-done((bf16[32,512]{1,0:T(8,128)(2,1)S(1)}, bf16[32,512]{1,0:T(8,128)(2,1)}, u32[]{:S(2)}) %copy-start.2) | copy-done | bytes 32792
  4.0 0.0 copy-start.3
  4.0 0.8 %copy-done.3 = f32[4,2048]{1,0:T(4,128)S(1)} copy-done((f32[4,2048]{1,0:T(4,128)S(1)}, f32[4,2048]{1,0:T(4,128)}, u32[]{:S(2)}) %copy-start.3) | copy-done | bytes 32792
  4.7 0.0 copy-start.4
  4.8 0.7 copy-done.4
  5.4 0.0 copy-start.5
  5.4 0.7 copy-done.5
  6.1 0.0 copy-start.6
  6.1 0.7 copy-done.6
  6.8 36.3 %scan.1.n_ref = bf16[512,2048]{1,0:T(8,128)(2,1)S(1)} custom-call(bf16[512,2048]{1,0:T(8,128)(2,1)S(1)} %copy-done, bf16[512,256]{1,0:T(8,128)(2,1)S(1)} %bitcast.7, bf16[512,2048]{1,0:T(8,128)(2,1)} %z_ref.1, bf16[32,512]{1,0:T(8,128)(2,1)S(1)} %copy-done.2, f32[1,32]{1,0:T(1,128)S(1)} %bitcast.10, f32[4,2048]{1,0:T(4,128)S(1)} %copy-done.3, ...), custom_call_target="tpu_custom_call" | custom-call | tf_op jit(solution)/shard_map/scan/pallas_call | solution.py:371
  43.1 29.4 %project.1 = bf16[1024,512]{1,0:T(8,128)(2,1)S(1)} custom-call(bf16[512,2048]{1,0:T(8,128)(2,1)S(1)} %scan.1.n_ref, bf16[2048,4096]{1,0:T(8,128)(2,1)} %w_ref.1), custom_call_target="tpu_custom_call" | custom-call | tf_op jit(solution)/shard_map/project/pallas_call | solution.py:428
  72.5 1.0 %copy.15 = bf16[1024,512]{1,0:T(8,128)(2,1)} copy(bf16[1024,512]{1,0:T(8,128)(2,1)S(1)} %project.1) | data formatting | bytes 2097152
Async XLA Ops:
  0.7 1.6 %copy-start = (bf16[512,2048]{1,0:T(8,128)(2,1)S(1)}, bf16[512,2048]{1,0:T(8,128)(2,1)}, u32[]{:S(2)}) copy-start(bf16[512,2048]{1,0:T(8,128)(2,1)} %x_ref.1) | copy-start | bytes 6291460
  2.3 0.9 %copy-start.1 = (bf16[512,1,256]{2,0,1:T(8,128)(2,1)S(1)}, bf16[512,1,256]{2,0,1:T(8,128)(2,1)}, u32[]{:S(2)}) copy-start(bf16[512,1,256]{2,0,1:T(8,128)(2,1)} %param.11) | copy-start | bytes 786436
  3.2 0.8 %copy-start.2 = (bf16[32,512]{1,0:T(8,128)(2,1)S(1)}, bf16[32,512]{1,0:T(8,128)(2,1)}, u32[]{:S(2)}) copy-start(bf16[32,512]{1,0:T(8,128)(2,1)} %dt_ref.1) | copy-start | bytes 98308
  4.0 0.8 %copy-start.3 = (f32[4,2048]{1,0:T(4,128)S(1)}, f32[4,2048]{1,0:T(4,128)}, u32[]{:S(2)}) copy-start(f32[4,2048]{1,0:T(4,128)} %cx_ref.1) | copy-start | bytes 98308
  4.7 0.7 copy-start.4
  5.4 0.7 copy-start.5
  6.1 0.7 copy-start.6

commit v2 on v1

v2 whole, which is shorter than its diff:
```python
import functools

import jax
import jax.numpy as jnp
from jax import lax
from jax.experimental import pallas as pl
from jax.experimental.pallas import tpu as pltpu
from jax.sharding import PartitionSpec as P

SPAN = 128
MESH = pl.DeviceIdType.MESH
F32 = jnp.float32
BF16 = jnp.bfloat16
LANES = 256
RIM = 16


def half_tanh_silu(u):
    return 0.5 * u * (1.0 + jnp.tanh(0.5 * u))


def conv_silu(before, now, taps):
    cat = jnp.concatenate([before.astype(F32), now.astype(F32)], 0)
    width = taps.shape[0]
    total = taps[width - 1 : width] * cat[RIM:]
    for k in range(width - 1):
        total = total + taps[k : k + 1] * pltpu.roll(cat, width - 1 - k, 0)[RIM:]
    return half_tanh_silu(total)


def layer_kernel(
    n_seq, x_hbm, bc_hbm, z_hbm, dt_hbm, alog_hbm, cx_hbm, cbc_hbm, skip_hbm, gain_hbm, w_hbm, out_hbm,
    x_ref, bc_ref, z_ref, dt_ref, alog_ref, cx_ref, cbc_ref, skip_ref, gain_ref, w_buf,
    halo_x, halo_bc, xconv, b_t, c_mat, score, ld_row, st_row, ld_col, t_tail, t_exp, pick,
    decay_in, decay_blk, decay_own, decay_other, skip_row, local_in, final, y_ref, enter,
    y_send, y_recv, z_send, z_recv, n_buf, s1, r1, s2, r2, s3, r3, keep, o_buf,
    in_sem, w_sem, halo_sems, dec_sems, ys_sem, yr_sem, zs_sem, zr_sem,
    s1s, s1r, s2s, s2r, s3s, s3r, o_sem,
):
    tokens, inner = x_ref.shape
    heads = dt_ref.shape[0]
    state = b_t.shape[1]
    width = inner // heads
    blocks = tokens // SPAN
    chunks = inner // LANES
    per = heads // chunks
    rows = n_seq // 2
    pieces, cols = keep.shape[0], keep.shape[2]
    half = tokens // 2
    q = lax.axis_index("seq")
    odd = lax.rem(q, 2)
    place = q // 2
    pair = q + 1 - 2 * odd
    after = lax.rem(q + 1, n_seq)
    ahead = lax.rem(q + 2, n_seq)
    h = lax.axis_index("head")
    core = lax.rem(h, 2)
    side = h // 2
    near = 2 * side + 1 - core
    far = 2 * (1 - side) + core
    cross = 3 - h

    loads = [
        pltpu.make_async_copy(src, dst, in_sem.at[i])
        for i, (src, dst) in enumerate(
            [
                (dt_hbm, dt_ref), (alog_hbm, alog_ref), (skip_hbm, skip_ref), (bc_hbm, bc_ref), (cbc_hbm, cbc_ref),
                (cx_hbm, cx_ref), (x_hbm, x_ref), (gain_hbm, gain_ref), (z_hbm, z_ref),
            ]
        )
    ]
    for load in loads:
        load.start()

    barrier = pltpu.get_barrier_semaphore()
    pl.semaphore_signal(barrier, inc=1, device_id={"seq": pair}, device_id_type=MESH)
    for other in (near, far):
        pl.semaphore_signal(barrier, inc=1, device_id={"head": other}, device_id_type=MESH)

    @pl.when(q > 0)
    def _():
        pl.semaphore_signal(barrier, inc=1, device_id={"seq": q - 1}, device_id_type=MESH)

    @pl.when(q > 1)
    def _():
        pl.semaphore_signal(barrier, inc=1, device_id={"seq": q - 2}, device_id_type=MESH)

    def fetch(block, c, slot):
        start = pl.multiple_of((block * pieces + c) * cols, cols)
        return pltpu.make_async_copy(w_hbm.at[:, pl.ds(start, cols)], w_buf.at[slot], w_sem.at[slot])

    def fetch_all(act):
        def one(c, carry):
            act(fetch(cross, c, c))
            act(fetch(far, c, pieces + c))
            act(fetch(near, c, 2 * pieces + c))
            act(fetch(h, c, 3 * pieces + c))
            return carry

        lax.fori_loop(0, pieces, one, 0)

    fetch_all(lambda copy: copy.start())

    peers = 3 + jnp.minimum(n_seq - 1 - q, 1) + jnp.minimum(jnp.maximum(n_seq - 2 - q, 0), 1)
    pl.semaphore_wait(barrier, peers)

    def send(src, dst, s, r, to):
        return pltpu.make_async_remote_copy(
            src_ref=src, dst_ref=dst, send_sem=s, recv_sem=r, device_id=to, device_id_type=MESH
        )

    halo_copies = [
        send(bc_hbm.at[pl.ds(tokens - RIM, RIM)], halo_bc, halo_sems.at[2], halo_sems.at[3], {"seq": after}),
        send(x_hbm.at[pl.ds(tokens - RIM, RIM)], halo_x, halo_sems.at[0], halo_sems.at[1], {"seq": after}),
    ]

    @pl.when(q < n_seq - 1)
    def _():
        for copy in halo_copies:
            copy.start()

    r_id = lax.broadcasted_iota(jnp.int32, (SPAN, SPAN), 0)
    c_id = lax.broadcasted_iota(jnp.int32, (SPAN, SPAN), 1)
    upto = jnp.where(r_id <= c_id, 1.0, 0.0).astype(F32)
    hr = lax.broadcasted_iota(jnp.int32, (heads, heads), 0)
    hc = lax.broadcasted_iota(jnp.int32, (heads, heads), 1)
    lane_head = lax.shift_right_logical(
        lax.broadcasted_iota(jnp.int32, (heads, inner), 1), jnp.full((heads, inner), width.bit_length() - 1, jnp.int32)
    )
    mine = lax.broadcasted_iota(jnp.int32, (heads, inner), 0) == lane_head
    ones = jnp.where(mine, 1.0, 0.0).astype(F32)
    pick[...] = jnp.concatenate([ones, ones], 0).astype(BF16)
    for load in loads[:3]:
        load.wait()
    neg_a = -jnp.sum(jnp.where(hr == hc, jnp.exp(alog_ref[...]), 0.0), axis=1, keepdims=True)
    skips = jnp.sum(jnp.where(hr == hc, jnp.broadcast_to(skip_ref[...], (heads, heads)), 0.0), axis=1, keepdims=True)
    skip_row[...] = jnp.broadcast_to(jnp.sum(ones * skips, axis=0, keepdims=True), (8, inner))
    dt = jnp.concatenate([dt_ref[:, b * SPAN : (b + 1) * SPAN].astype(F32) for b in range(blocks)], 0)
    e = jnp.exp(-jnp.abs(dt))
    log1p = jnp.where(e < 0.01, e * (1.0 - e * (0.5 - e * (1.0 / 3.0 - 0.25 * e))), jnp.log(1.0 + e))
    step = jnp.maximum(dt, 0.0) + log1p
    rate = jnp.concatenate([neg_a] * blocks, 0) * step
    ld = jnp.dot(rate, upto, preferred_element_type=F32, precision=lax.Precision.HIGHEST)
    tail = jnp.exp(ld[:, SPAN - 1 : SPAN] - ld) * step
    grow = jnp.exp(ld)

    def turned_pieces(value):
        high = value.astype(BF16).astype(F32)
        low = value - high
        parts = []
        for b in range(blocks):
            parts += [high[b * heads : (b + 1) * heads], low[b * heads : (b + 1) * heads]]
        turned = jnp.concatenate(parts, 0).T
        return [turned[:, 2 * heads * b : 2 * heads * (b + 1)].astype(BF16) for b in range(blocks)]

    tails, grows, turned = turned_pieces(tail), turned_pieces(grow), ld.T
    running = jnp.ones((8, inner), F32)
    for b in range(blocks):
        t_tail[b] = tails[b]
        t_exp[b] = grows[b]
        for c in range(chunks):
            at = b * heads + c * per
            ld_row[b, c] = ld[at : at + per]
            st_row[b, c] = step[at : at + per]
            ld_col[b, c] = turned[:, at : at + per]
        last = jnp.sum(ones * grow[b * heads : (b + 1) * heads, SPAN - 1 : SPAN], axis=0, keepdims=True)
        decay_in[b] = running
        decay_blk[b] = jnp.broadcast_to(last, (8, inner))
        running = running * last
    decay_own[...] = running
    dec_copy = send(decay_own, decay_other, dec_sems.at[0], dec_sems.at[1], {"seq": pair})
    dec_copy.start()
    for load in loads[3:7]:
        load.wait()

    @pl.when(q > 0)
    def _():
        for copy in halo_copies:
            copy.wait_recv()

    @pl.when(q == 0)
    def _():
        halo_x[...] = jnp.zeros_like(halo_x)
        halo_bc[...] = jnp.zeros_like(halo_bc)

    for b in range(blocks):
        before = halo_bc[...] if b == 0 else bc_ref[b * SPAN - RIM : b * SPAN]
        bc = conv_silu(before, bc_ref[b * SPAN : (b + 1) * SPAN], cbc_ref[...])
        b_f = bc[:, :state].astype(BF16)
        c_f = bc[:, state:].astype(BF16)
        b_t[b] = bc[:, :state].T.astype(BF16)
        c_mat[b] = c_f
        sc = lax.dot_general(c_f, b_f, (((1,), (1,)), ((), ())), preferred_element_type=F32)
        score[b] = jnp.where(r_id >= c_id, sc, 0.0)

    def y_copy(c):
        return send(y_send.at[c], y_recv.at[c], ys_sem.at[c], yr_sem.at[c], {"seq": pair})

    def z_copy(c):
        return send(z_send.at[c], z_recv.at[c], zs_sem.at[c], zr_sem.at[c], {"seq": ahead})

    def state_chunk(c, carry):
        lanes = pl.ds(pl.multiple_of(c * LANES, LANES), LANES)
        held = jnp.zeros((state, LANES), F32)
        for b in range(blocks):
            tail = jnp.dot(t_tail[b], pick[:, lanes], preferred_element_type=F32)
            before = halo_x[:, lanes] if b == 0 else x_ref[pl.ds(b * SPAN - RIM, RIM), lanes]
            xc = conv_silu(before, x_ref[pl.ds(b * SPAN, SPAN), lanes], cx_ref[:, lanes]).astype(BF16)
            xconv[pl.ds(b * SPAN, SPAN), lanes] = xc
            weighted = (xc.astype(F32) * tail).astype(BF16)
            local_in[b, :, lanes] = held
            new = jnp.dot(b_t[b], weighted, preferred_element_type=F32)
            held = decay_blk[b, 0:1, lanes] * held + new
        final[:, lanes] = held
        y_send[c] = held.astype(BF16)
        y_copy(c).start()
        return carry

    lax.fori_loop(0, chunks, state_chunk, 0)
    dec_copy.wait_recv()
    is_odd = odd.astype(F32)

    def serve(c):
        lanes = pl.ds(pl.multiple_of(c * LANES, LANES), LANES)
        y_copy(c).wait_recv()
        own = final[:, lanes]
        other = y_recv[c].astype(F32)
        d_own = decay_own[0:1, lanes]
        d_other = decay_other[0:1, lanes]
        enter[:, lanes] = is_odd * other

        @pl.when(place < rows - 1)
        def _():
            final[:, lanes] = own * (is_odd + (1.0 - is_odd) * d_other) + other * (1.0 - is_odd + is_odd * d_own)

        @pl.when(place > 0)
        def _():
            z_copy(c).wait_recv()

            @pl.when(place < rows - 1)
            def _():
                final[:, lanes] += d_own * d_other * z_recv[c].astype(F32)

        @pl.when(place < rows - 1)
        def _():
            z_send[c] = final[:, lanes].astype(BF16)
            z_copy(c).start()

        @pl.when(place > 0)
        def _():
            enter[:, lanes] += z_recv[c].astype(F32) * (1.0 - is_odd + is_odd * d_other)

    first_head = lax.broadcasted_iota(jnp.int32, (1, 2 * width), 1) < width
    left = jnp.where(first_head, 1.0, 0.0).astype(BF16)
    right = jnp.where(first_head, 0.0, 1.0).astype(BF16)

    def intra(c):
        for b in range(blocks):
            token = pl.ds(b * SPAN, SPAN)
            lds = ld_row[b, c]
            sts = st_row[b, c]
            cl = ld_col[b, c]
            for j in range(per // 2):
                lanes = pl.ds(pl.multiple_of(c * LANES + j * 2 * width, 2 * width), 2 * width)
                mixes = []
                for i in (2 * j, 2 * j + 1):
                    gap = jnp.minimum(cl[:, i : i + 1] - lds[i : i + 1], 0.0)
                    mixes.append((score[b] * jnp.exp(gap) * sts[i : i + 1]).astype(BF16))
                xc = xconv[token, lanes]
                y_ref[token, lanes] = jnp.dot(
                    jnp.concatenate(mixes, 1),
                    jnp.concatenate([xc * left, xc * right], 0),
                    preferred_element_type=F32,
                )

    def slot(j, carry):
        c = j - place

        @pl.when((c >= 0) & (c < chunks))
        def _():
            serve(c)

        @pl.when(j < chunks)
        def _():
            intra(j)

        return carry

    lax.fori_loop(0, chunks + rows - 1, slot, 0)
    for load in loads[7:]:
        load.wait()
    fetch_all(lambda copy: copy.wait())

    def finish(b, carry):
        token = pl.ds(pl.multiple_of(b * SPAN, SPAN), SPAN)
        power = jnp.zeros((SPAN, 1), F32)
        for c in range(chunks):
            lanes = pl.ds(c * LANES, LANES)
            grown = jnp.dot(t_exp[b], pick[:, lanes], preferred_element_type=F32)
            ent = (local_in[b, :, lanes] + decay_in[b, 0:1, lanes] * enter[:, lanes]).astype(BF16)
            read = jnp.dot(c_mat[b], ent, preferred_element_type=F32)
            total = y_ref[token, lanes] + grown * read + skip_row[0:1, lanes] * xconv[token, lanes].astype(F32)
            gated = total * half_tanh_silu(z_ref[token, lanes].astype(F32))
            y_ref[token, lanes] = gated
            power = power + jnp.sum(gated * gated, axis=1, keepdims=True)
        scale = lax.rsqrt(power * (1.0 / inner) + 1e-05)
        for c in range(chunks):
            lanes = pl.ds(c * LANES, LANES)
            n_buf[token, lanes] = (y_ref[token, lanes] * scale * gain_ref[:, lanes]).astype(BF16)
        return carry

    def near_copy(src, dst, s, r, i):
        return send(src.at[i], dst.at[i], s.at[i], r.at[i], {"head": near})

    def far_copy(i):
        return send(s2.at[i], r2.at[i], s2s.at[i], s2r.at[i], {"head": far})

    def first(part, c):
        i = part * pieces + c
        token = pl.ds(pl.multiple_of(part * half, half), half)
        s1[i] = jnp.dot(n_buf[token, :], w_buf[c], preferred_element_type=F32).astype(BF16)
        near_copy(s1, r1, s1s, s1r, i).start()
        summed = jnp.dot(n_buf[token, :], w_buf[pieces + c], preferred_element_type=F32)
        near_copy(s1, r1, s1s, s1r, i).wait_recv()
        s2[i] = (summed + r1[i].astype(F32)).astype(BF16)
        far_copy(i).start()

    def one_half(part, carry):
        lax.fori_loop(part * (blocks // 2), (part + 1) * (blocks // 2), finish, 0)

        def piece(c, carry):
            first(part, c)
            return carry

        return lax.fori_loop(0, pieces, piece, carry)

    def second(c, carry):
        s3[c] = jnp.dot(n_buf[...], w_buf[2 * pieces + c], preferred_element_type=F32).astype(BF16)
        near_copy(s3, r3, s3s, s3r, c).start()
        keep[c] = jnp.dot(n_buf[...], w_buf[3 * pieces + c], preferred_element_type=F32)
        return carry

    def third(c, carry):
        near_copy(s3, r3, s3s, s3r, c).wait_recv()
        keep[c] += r3[c].astype(F32)
        return carry

    def store(part, c):
        place_out = (
            pl.ds(pl.multiple_of(c * cols, cols), cols),
            pl.ds(pl.multiple_of(part * half, half), half),
        )
        return pltpu.make_async_copy(
            o_buf.at[part * pieces + c], out_hbm.at[place_out[0], place_out[1]], o_sem.at[part * pieces + c]
        )

    def fourth(part, carry):
        def piece(c, carry):
            i = part * pieces + c
            far_copy(i).wait_recv()
            total = keep[c, pl.ds(pl.multiple_of(part * half, half), half), :] + r2[i].astype(F32)
            o_buf[i] = total.T.astype(BF16)
            store(part, c).start()
            return carry

        return lax.fori_loop(0, pieces, piece, carry)

    lax.fori_loop(0, 2, one_half, 0)
    lax.fori_loop(0, pieces, second, 0)
    lax.fori_loop(0, pieces, third, 0)
    lax.fori_loop(0, 2, fourth, 0)

    dec_copy.wait_send()

    @pl.when(q < n_seq - 1)
    def _():
        for copy in halo_copies:
            copy.wait_send()

    def drain_state(c, carry):
        y_copy(c).wait_send()

        @pl.when(place < rows - 1)
        def _():
            z_copy(c).wait_send()

        return carry

    def drain_first(i, carry):
        near_copy(s1, r1, s1s, s1r, i).wait_send()
        far_copy(i).wait_send()
        return carry

    def drain_second(c, carry):
        near_copy(s3, r3, s3s, s3r, c).wait_send()
        store(0, c).wait()
        store(1, c).wait()
        return carry

    lax.fori_loop(0, chunks, drain_state, 0)
    lax.fori_loop(0, 2 * pieces, drain_first, 0)
    lax.fori_loop(0, pieces, drain_second, 0)


def on_device(n_seq, x_in, bc_in, z_in, dt_raw, a_log, conv_x, conv_bc, d_skip, norm_gain, out_weight):
    tokens, inner = x_in.shape
    heads = dt_raw.shape[0]
    features = out_weight.shape[1]
    state = bc_in.shape[2] // 2
    taps = conv_x.shape[0]
    blocks = tokens // SPAN
    chunks = inner // LANES
    per = heads // chunks
    share = features // 4
    cols = min(256, share)
    pieces = share // cols
    hbm = pl.BlockSpec(memory_space=pl.ANY)
    dma = pltpu.SemaphoreType.DMA
    vmem = pltpu.VMEM
    halves = vmem((2 * pieces, tokens // 2, cols), BF16)
    wholes = vmem((pieces, tokens, cols), BF16)
    moved = vmem((chunks, state, LANES), BF16)
    return pl.pallas_call(
        functools.partial(layer_kernel, n_seq),
        name="layer",
        out_shape=jax.ShapeDtypeStruct((share, tokens), BF16),
        in_specs=[hbm] * 10,
        out_specs=hbm,
        scratch_shapes=[
            vmem((tokens, inner), BF16),
            vmem((tokens, 2 * state), BF16),
            vmem((tokens, inner), BF16),
            vmem((heads, tokens), BF16),
            vmem((1, heads), F32),
            vmem((taps, inner), F32),
            vmem((taps, 2 * state), F32),
            vmem((1, heads), F32),
            vmem((1, inner), F32),
            vmem((4 * pieces, inner, cols), BF16),
            vmem((RIM, inner), BF16),
            vmem((RIM, 2 * state), BF16),
            vmem((tokens, inner), BF16),
            vmem((blocks, state, SPAN), BF16),
            vmem((blocks, SPAN, state), BF16),
            vmem((blocks, SPAN, SPAN), F32),
            vmem((blocks, chunks, per, SPAN), F32),
            vmem((blocks, chunks, per, SPAN), F32),
            vmem((blocks, chunks, SPAN, per), F32),
            vmem((blocks, SPAN, 2 * heads), BF16),
            vmem((blocks, SPAN, 2 * heads), BF16),
            vmem((2 * heads, inner), BF16),
            vmem((blocks, 8, inner), F32),
            vmem((blocks, 8, inner), F32),
            vmem((8, inner), F32),
            vmem((8, inner), F32),
            vmem((8, inner), F32),
            vmem((blocks, state, inner), F32),
            vmem((state, inner), F32),
            vmem((tokens, inner), F32),
            vmem((state, inner), F32),
            moved,
            moved,
            moved,
            moved,
            vmem((tokens, inner), BF16),
            halves,
            halves,
            halves,
            halves,
            wholes,
            wholes,
            vmem((pieces, tokens, cols), F32),
            vmem((2 * pieces, cols, tokens // 2), BF16),
            dma((9,)),
            dma((4 * pieces,)),
            dma((4,)),
            dma((2,)),
            dma((chunks,)),
            dma((chunks,)),
            dma((chunks,)),
            dma((chunks,)),
            dma((2 * pieces,)),
            dma((2 * pieces,)),
            dma((2 * pieces,)),
            dma((2 * pieces,)),
            dma((pieces,)),
            dma((pieces,)),
            dma((2 * pieces,)),
        ],
        compiler_params=pltpu.CompilerParams(
            collective_id=0, has_side_effects=True, vmem_limit_bytes=60 * 2**20
        ),
    )(
        x_in,
        bc_in.reshape(tokens, 2 * state),
        z_in,
        dt_raw,
        a_log.reshape(1, heads),
        conv_x,
        conv_bc.reshape(taps, 2 * state),
        d_skip.reshape(1, heads),
        norm_gain.reshape(1, inner),
        out_weight,
    )


def solution(mesh):
    placed = (
        P("seq", "head"),
        P("seq", "head", None),
        P("seq", "head"),
        P("head", "seq"),
        P("head"),
        P(None, "head"),
        P(None, "head", None),
        P("head"),
        P("head"),
        P("head", None),
    )
    return jax.shard_map(
        functools.partial(on_device, mesh.shape["seq"]),
        mesh=mesh, in_specs=placed, out_specs=P("head", "seq"), check_vma=False,
    )
```

time: 73.9 us -> 66.9 us (0.905)
  local copies, waits for them, and re-layouts: 7.72 us -> 3.54 us
  Pallas kernels: 65.7 us -> 62.4 us
    unnamed x16 -> x2, local copies, waits for them, and re-layouts: 7.72 us -> 3.54 us
    pallas_call x2 -> x1, Pallas kernels: 65.7 us -> 62.4 us  [on_device(): pl.pallas_call(functools.partial(layer_kernel, n_seq), name='layer', out_...]
where the time goes in v2:
time: 66.9 us; the launch traced here: 65.9 us
  Pallas kernels  62.4 us (93%)
  local copies, waits for them, and re-layouts  3.54 us (5%)
    pallas_call x1, Pallas kernels, on_device(): pl.pallas_call(functools.partial(layer_kernel, n_seq), name='layer', out_...  62.4 us
    unnamed x2, local copies, waits for them, and re-layouts  3.54 us

profile of v2, /device:TPU:24, one launch (start us, length us, event | category | flops | bytes accessed | tf_op | source)
XLA Modules:
  0.0 65.9 jit_solution(9100806578252504952)
XLA Ops:
  0.0 1.3 %copy.13 = f32[4,1,256]{2,0,1:T(4,128)} copy(f32[4,1,256]{2,1,0:T(1,128)} %param.16) | data formatting | bytes 8192
  1.3 62.4 %layer.1 = bf16[1024,512]{1,0:T(8,128)(2,1)} custom-call(bf16[512,2048]{1,0:T(8,128)(2,1)} %x_hbm.1, bf16[512,256]{1,0:T(8,128)(2,1)} %bitcast.7, bf16[512,2048]{1,0:T(8,128)(2,1)} %z_hbm.1, bf16[32,512]{1,0:T(8,128)(2,1)} %dt_hbm.1, f32[1,32]{1,0:T(1,128)} %bitcast.10, f32[4,2048]{1,0:T(4,128)} %cx_hbm.1, f32[4,256]{1,0:T(4,128)} %bitcast.8, ...), custom_call_target="tpu_custom_call" | custom-call | tf_op jit(solution)/shard_map/layer/pallas_call | solution.py:423
  63.6 2.3 %copy.15 = bf16[1024,512]{1,0:T(8,128)(2,1)} copy(bf16[1024,512]{1,0:T(8,128)(2,1)} %layer.1) | data formatting | bytes 2097152

commit v3 on v2

--- a/solution.py
+++ b/solution.py
@@ -29,13 +29,13 @@
 
 
 def layer_kernel(
-    n_seq, x_hbm, bc_hbm, z_hbm, dt_hbm, alog_hbm, cx_hbm, cbc_hbm, skip_hbm, gain_hbm, w_hbm, out_hbm,
+    n_seq, x_hbm, bc_hbm, z_hbm, dt_hbm, alog_hbm, cx_hbm, cbc_hbm, skip_hbm, gain_hbm, w_hbm, out_ref,
     x_ref, bc_ref, z_ref, dt_ref, alog_ref, cx_ref, cbc_ref, skip_ref, gain_ref, w_buf,
     halo_x, halo_bc, xconv, b_t, c_mat, score, ld_row, st_row, ld_col, t_tail, t_exp, pick,
     decay_in, decay_blk, decay_own, decay_other, skip_row, local_in, final, y_ref, enter,
-    y_send, y_recv, z_send, z_recv, n_buf, s1, r1, s2, r2, s3, r3, keep, o_buf,
+    y_send, y_recv, z_send, z_recv, n_buf, s1, r1, s2, r2, s3, r3, keep,
     in_sem, w_sem, halo_sems, dec_sems, ys_sem, yr_sem, zs_sem, zr_sem,
-    s1s, s1r, s2s, s2r, s3s, s3r, o_sem,
+    s1s, s1r, s2s, s2r, s3s, s3r,
 ):
     tokens, inner = x_ref.shape
     heads = dt_ref.shape[0]
@@ -46,7 +46,6 @@
     per = heads // chunks
     rows = n_seq // 2
     pieces, cols = keep.shape[0], keep.shape[2]
-    half = tokens // 2
     q = lax.axis_index("seq")
     odd = lax.rem(q, 2)
     place = q // 2
@@ -98,8 +97,6 @@
             return carry
 
         lax.fori_loop(0, pieces, one, 0)
-
-    fetch_all(lambda copy: copy.start())
 
     peers = 3 + jnp.minimum(n_seq - 1 - q, 1) + jnp.minimum(jnp.maximum(n_seq - 2 - q, 0), 1)
     pl.semaphore_wait(barrier, peers)
@@ -172,6 +169,7 @@
     dec_copy.start()
     for load in loads[3:7]:
         load.wait()
+    fetch_all(lambda copy: copy.start())
 
     @pl.when(q > 0)
     def _():
@@ -183,9 +181,12 @@
         halo_x[...] = jnp.zeros_like(halo_x)
         halo_bc[...] = jnp.zeros_like(halo_bc)
 
+    taps_bc = jnp.concatenate(
+        [cbc_ref[:, k * 2 * state : (k + 1) * 2 * state] for k in range(cx_ref.shape[0])], 0
+    )
     for b in range(blocks):
         before = halo_bc[...] if b == 0 else bc_ref[b * SPAN - RIM : b * SPAN]
-        bc = conv_silu(before, bc_ref[b * SPAN : (b + 1) * SPAN], cbc_ref[...])
+        bc = conv_silu(before, bc_ref[b * SPAN : (b + 1) * SPAN], taps_bc)
         b_f = bc[:, :state].astype(BF16)
         c_f = bc[:, state:].astype(BF16)
         b_t[b] = bc[:, :state].T.astype(BF16)
@@ -199,7 +200,7 @@
     def z_copy(c):
         return send(z_send.at[c], z_recv.at[c], zs_sem.at[c], zr_sem.at[c], {"seq": ahead})
 
-    def state_chunk(c, carry):
+    def state_chunk(c):
         lanes = pl.ds(pl.multiple_of(c * LANES, LANES), LANES)
         held = jnp.zeros((state, LANES), F32)
         for b in range(blocks):
@@ -214,9 +215,7 @@
         final[:, lanes] = held
         y_send[c] = held.astype(BF16)
         y_copy(c).start()
-        return carry
-
-    lax.fori_loop(0, chunks, state_chunk, 0)
+
     dec_copy.wait_recv()
     is_odd = odd.astype(F32)
 
@@ -274,7 +273,7 @@
                 )
 
     def slot(j, carry):
-        c = j - place
+        c = j - 2 - 2 * place
 
         @pl.when((c >= 0) & (c < chunks))
         def _():
@@ -282,16 +281,20 @@
 
         @pl.when(j < chunks)
         def _():
-            intra(j)
-
-        return carry
-
-    lax.fori_loop(0, chunks + rows - 1, slot, 0)
+            state_chunk(j)
+
+        @pl.when((j >= chunks) & (j < 2 * chunks))
+        def _():
+            intra(j - chunks)
+
+        return carry
+
+    lax.fori_loop(0, max(2 * chunks, chunks + 2 * rows), slot, 0)
     for load in loads[7:]:
         load.wait()
     fetch_all(lambda copy: copy.wait())
 
-    def finish(b, carry):
+    def finish(b):
         token = pl.ds(pl.multiple_of(b * SPAN, SPAN), SPAN)
         power = jnp.zeros((SPAN, 1), F32)
         for c in range(chunks):
@@ -307,7 +310,6 @@
         for c in range(chunks):
             lanes = pl.ds(c * LANES, LANES)
             n_buf[token, lanes] = (y_ref[token, lanes] * scale * gain_ref[:, lanes]).astype(BF16)
-        return carry
 
     def near_copy(src, dst, s, r, i):
         return send(src.at[i], dst.at[i], s.at[i], r.at[i], {"head": near})
@@ -315,24 +317,27 @@
     def far_copy(i):
         return send(s2.at[i], r2.at[i], s2s.at[i], s2r.at[i], {"head": far})
 
-    def first(part, c):
-        i = part * pieces + c
-        token = pl.ds(pl.multiple_of(part * half, half), half)
-        s1[i] = jnp.dot(n_buf[token, :], w_buf[c], preferred_element_type=F32).astype(BF16)
-        near_copy(s1, r1, s1s, s1r, i).start()
-        summed = jnp.dot(n_buf[token, :], w_buf[pieces + c], preferred_element_type=F32)
-        near_copy(s1, r1, s1s, s1r, i).wait_recv()
-        s2[i] = (summed + r1[i].astype(F32)).astype(BF16)
-        far_copy(i).start()
-
-    def one_half(part, carry):
-        lax.fori_loop(part * (blocks // 2), (part + 1) * (blocks // 2), finish, 0)
-
-        def piece(c, carry):
-            first(part, c)
+    def one_part(part, carry):
+        token = pl.ds(pl.multiple_of(part * SPAN, SPAN), SPAN)
+        finish(part)
+
+        def pair_piece(c, carry):
+            i = part * pieces + c
+            s1[i] = jnp.dot(n_buf[token, :], w_buf[c], preferred_element_type=F32).astype(BF16)
+            near_copy(s1, r1, s1s, s1r, i).start()
             return carry
 
-        return lax.fori_loop(0, pieces, piece, carry)
+        def far_piece(c, carry):
+            i = part * pieces + c
+            summed = jnp.dot(n_buf[token, :], w_buf[pieces + c], preferred_element_type=F32)
+            near_copy(s1, r1, s1s, s1r, i).wait_recv()
+            s2[i] = (summed + r1[i].astype(F32)).astype(BF16)
+            far_copy(i).start()
+            return carry
+
+        lax.fori_loop(0, pieces, pair_piece, 0)
+        lax.fori_loop(0, pieces, far_piece, 0)
+        return carry
 
     def second(c, carry):
         s3[c] = jnp.dot(n_buf[...], w_buf[2 * pieces + c], preferred_element_type=F32).astype(BF16)
@@ -345,30 +350,22 @@
         keep[c] += r3[c].astype(F32)
         return carry
 
-    def store(part, c):
-        place_out = (
-            pl.ds(pl.multiple_of(c * cols, cols), cols),
-            pl.ds(pl.multiple_of(part * half, half), half),
-        )
-        return pltpu.make_async_copy(
-            o_buf.at[part * pieces + c], out_hbm.at[place_out[0], place_out[1]], o_sem.at[part * pieces + c]
-        )
-
     def fourth(part, carry):
+        token = pl.ds(pl.multiple_of(part * SPAN, SPAN), SPAN)
+
         def piece(c, carry):
             i = part * pieces + c
             far_copy(i).wait_recv()
-            total = keep[c, pl.ds(pl.multiple_of(part * half, half), half), :] + r2[i].astype(F32)
-            o_buf[i] = total.T.astype(BF16)
-            store(part, c).start()
+            total = keep[c, token, :] + r2[i].astype(F32)
+            out_ref[pl.ds(pl.multiple_of(c * cols, cols), cols), token] = total.T.astype(BF16)
             return carry
 
         return lax.fori_loop(0, pieces, piece, carry)
 
-    lax.fori_loop(0, 2, one_half, 0)
+    lax.fori_loop(0, blocks, one_part, 0)
     lax.fori_loop(0, pieces, second, 0)
     lax.fori_loop(0, pieces, third, 0)
-    lax.fori_loop(0, 2, fourth, 0)
+    lax.fori_loop(0, blocks, fourth, 0)
 
     dec_copy.wait_send()
 
@@ -393,12 +390,10 @@
 
     def drain_second(c, carry):
         near_copy(s3, r3, s3s, s3r, c).wait_send()
-        store(0, c).wait()
-        store(1, c).wait()
         return carry
 
     lax.fori_loop(0, chunks, drain_state, 0)
-    lax.fori_loop(0, 2 * pieces, drain_first, 0)
+    lax.fori_loop(0, blocks * pieces, drain_first, 0)
     lax.fori_loop(0, pieces, drain_second, 0)
 
 
@@ -417,7 +412,7 @@
     hbm = pl.BlockSpec(memory_space=pl.ANY)
     dma = pltpu.SemaphoreType.DMA
     vmem = pltpu.VMEM
-    halves = vmem((2 * pieces, tokens // 2, cols), BF16)
+    parts = vmem((blocks * pieces, SPAN, cols), BF16)
     wholes = vmem((pieces, tokens, cols), BF16)
     moved = vmem((chunks, state, LANES), BF16)
     return pl.pallas_call(
@@ -425,7 +420,7 @@
         name="layer",
         out_shape=jax.ShapeDtypeStruct((share, tokens), BF16),
         in_specs=[hbm] * 10,
-        out_specs=hbm,
+        out_specs=pl.BlockSpec(memory_space=pltpu.VMEM),
         scratch_shapes=[
             vmem((tokens, inner), BF16),
             vmem((tokens, 2 * state), BF16),
@@ -433,7 +428,7 @@
             vmem((heads, tokens), BF16),
             vmem((1, heads), F32),
             vmem((taps, inner), F32),
-            vmem((taps, 2 * state), F32),
+            vmem((1, taps * 2 * state), F32),
             vmem((1, heads), F32),
             vmem((1, inner), F32),
             vmem((4 * pieces, inner, cols), BF16),
@@ -463,14 +458,13 @@
             moved,
             moved,
             vmem((tokens, inner), BF16),
-            halves,
-            halves,
-            halves,
-            halves,
+            parts,
+            parts,
+            parts,
+            parts,
             wholes,
             wholes,
             vmem((pieces, tokens, cols), F32),
-            vmem((2 * pieces, cols, tokens // 2), BF16),
             dma((9,)),
             dma((4 * pieces,)),
             dma((4,)),
@@ -479,13 +473,12 @@
             dma((chunks,)),
             dma((chunks,)),
             dma((chunks,)),
-            dma((2 * pieces,)),
-            dma((2 * pieces,)),
-            dma((2 * pieces,)),
-            dma((2 * pieces,)),
+            dma((blocks * pieces,)),
+            dma((blocks * pieces,)),
+            dma((blocks * pieces,)),
+            dma((blocks * pieces,)),
             dma((pieces,)),
             dma((pieces,)),
-            dma((2 * pieces,)),
         ],
         compiler_params=pltpu.CompilerParams(
             collective_id=0, has_side_effects=True, vmem_limit_bytes=60 * 2**20
@@ -497,7 +490,7 @@
         dt_raw,
         a_log.reshape(1, heads),
         conv_x,
-        conv_bc.reshape(taps, 2 * state),
+        conv_bc.reshape(1, taps * 2 * state),
         d_skip.reshape(1, heads),
         norm_gain.reshape(1, inner),
         out_weight,

time: 66.9 us -> 65.8 us (0.984); the launches traced: 65.9 us -> 65.7 us
  local copies, waits for them, and re-layouts: 3.54 us -> 2.26 us
  Pallas kernels: 62.4 us -> 63.4 us
    unnamed x2 -> x1, local copies, waits for them, and re-layouts: 3.54 us -> 2.26 us
    pallas_call x1, Pallas kernels: 62.4 us -> 63.4 us  [on_device(): pl.pallas_call(functools.partial(layer_kernel, n_seq), name='layer', out_...]
where the time goes in v3:
time: 65.8 us; the launch traced here: 65.7 us
  Pallas kernels  63.4 us (96%)
  local copies, waits for them, and re-layouts  2.26 us (3%)
    pallas_call x1, Pallas kernels, on_device(): pl.pallas_call(functools.partial(layer_kernel, n_seq), name='layer', out_...  63.4 us
    unnamed x1, local copies, waits for them, and re-layouts  2.26 us

profile of v3, /device:TPU:24, one launch (start us, length us, event | category | flops | bytes accessed | tf_op | source)
XLA Modules:
  0.0 65.7 jit_solution(408440918927697177)
XLA Ops:
  0.0 63.4 %layer.1 = bf16[1024,512]{1,0:T(8,128)(2,1)} custom-call(bf16[512,2048]{1,0:T(8,128)(2,1)} %x_hbm.1, bf16[512,256]{1,0:T(8,128)(2,1)} %bitcast.5, bf16[512,2048]{1,0:T(8,128)(2,1)} %z_hbm.1, bf16[32,512]{1,0:T(8,128)(2,1)} %dt_hbm.1, f32[1,32]{1,0:T(1,128)} %bitcast.8, f32[4,2048]{1,0:T(4,128)} %cx_hbm.1, f32[1,1024]{1,0:T(1,128)} %bitcast.7, ...), custom_call_target="tpu_custom_call" | custom-call | tf_op jit(solution)/shard_map/layer/pallas_call | solution.py:418
  63.4 2.3 %copy.12 = bf16[1024,512]{1,0:T(8,128)(2,1)} copy(bf16[1024,512]{1,0:T(8,128)(2,1)} %layer.1) | data formatting | bytes 2097152

commit v4 on v3

--- a/solution.py
+++ b/solution.py
@@ -31,9 +31,9 @@
 def layer_kernel(
     n_seq, x_hbm, bc_hbm, z_hbm, dt_hbm, alog_hbm, cx_hbm, cbc_hbm, skip_hbm, gain_hbm, w_hbm, out_ref,
     x_ref, bc_ref, z_ref, dt_ref, alog_ref, cx_ref, cbc_ref, skip_ref, gain_ref, w_buf,
-    halo_x, halo_bc, xconv, b_t, c_mat, score, ld_row, st_row, ld_col, t_tail, t_exp, pick,
+    halo_x, halo_bc, xconv, b_t, b_mat, c_mat, score, ld_row, st_row, ld_col, t_tail, t_exp, pick,
     decay_in, decay_blk, decay_own, decay_other, skip_row, local_in, final, y_ref, enter,
-    y_send, y_recv, z_send, z_recv, n_buf, s1, r1, s2, r2, s3, r3, keep,
+    y_send, y_recv, z_send, z_recv, s1, r1, s2, r2, s3, r3, keep,
     in_sem, w_sem, halo_sems, dec_sems, ys_sem, yr_sem, zs_sem, zr_sem,
     s1s, s1r, s2s, s2r, s3s, s3r,
 ):
@@ -124,14 +124,12 @@
     lane_head = lax.shift_right_logical(
         lax.broadcasted_iota(jnp.int32, (heads, inner), 1), jnp.full((heads, inner), width.bit_length() - 1, jnp.int32)
     )
-    mine = lax.broadcasted_iota(jnp.int32, (heads, inner), 0) == lane_head
-    ones = jnp.where(mine, 1.0, 0.0).astype(F32)
+    owner = lax.broadcasted_iota(jnp.int32, (heads, inner), 0) == lane_head
+    ones = jnp.where(owner, 1.0, 0.0).astype(F32)
     pick[...] = jnp.concatenate([ones, ones], 0).astype(BF16)
     for load in loads[:3]:
         load.wait()
     neg_a = -jnp.sum(jnp.where(hr == hc, jnp.exp(alog_ref[...]), 0.0), axis=1, keepdims=True)
-    skips = jnp.sum(jnp.where(hr == hc, jnp.broadcast_to(skip_ref[...], (heads, heads)), 0.0), axis=1, keepdims=True)
-    skip_row[...] = jnp.broadcast_to(jnp.sum(ones * skips, axis=0, keepdims=True), (8, inner))
     dt = jnp.concatenate([dt_ref[:, b * SPAN : (b + 1) * SPAN].astype(F32) for b in range(blocks)], 0)
     e = jnp.exp(-jnp.abs(dt))
     log1p = jnp.where(e < 0.01, e * (1.0 - e * (0.5 - e * (1.0 / 3.0 - 0.25 * e))), jnp.log(1.0 + e))
@@ -150,16 +148,10 @@
         turned = jnp.concatenate(parts, 0).T
         return [turned[:, 2 * heads * b : 2 * heads * (b + 1)].astype(BF16) for b in range(blocks)]
 
-    tails, grows, turned = turned_pieces(tail), turned_pieces(grow), ld.T
+    tails = turned_pieces(tail)
     running = jnp.ones((8, inner), F32)
     for b in range(blocks):
         t_tail[b] = tails[b]
-        t_exp[b] = grows[b]
-        for c in range(chunks):
-            at = b * heads + c * per
-            ld_row[b, c] = ld[at : at + per]
-            st_row[b, c] = step[at : at + per]
-            ld_col[b, c] = turned[:, at : at + per]
         last = jnp.sum(ones * grow[b * heads : (b + 1) * heads, SPAN - 1 : SPAN], axis=0, keepdims=True)
         decay_in[b] = running
         decay_blk[b] = jnp.broadcast_to(last, (8, inner))
@@ -191,8 +183,7 @@
         c_f = bc[:, state:].astype(BF16)
         b_t[b] = bc[:, :state].T.astype(BF16)
         c_mat[b] = c_f
-        sc = lax.dot_general(c_f, b_f, (((1,), (1,)), ((), ())), preferred_element_type=F32)
-        score[b] = jnp.where(r_id >= c_id, sc, 0.0)
+        b_mat[b] = b_f
 
     def y_copy(c):
         return send(y_send.at[c], y_recv.at[c], ys_sem.at[c], yr_sem.at[c], {"seq": pair})
@@ -200,7 +191,10 @@
     def z_copy(c):
         return send(z_send.at[c], z_recv.at[c], zs_sem.at[c], zr_sem.at[c], {"seq": ahead})
 
-    def state_chunk(c):
+    mine_count = chunks // 2
+
+    def state_chunk(j, carry):
+        c = lax.rem((1 - odd) * mine_count + j, chunks)
         lanes = pl.ds(pl.multiple_of(c * LANES, LANES), LANES)
         held = jnp.zeros((state, LANES), F32)
         for b in range(blocks):
@@ -213,19 +207,40 @@
             new = jnp.dot(b_t[b], weighted, preferred_element_type=F32)
             held = decay_blk[b, 0:1, lanes] * held + new
         final[:, lanes] = held
-        y_send[c] = held.astype(BF16)
-        y_copy(c).start()
-
+
+        @pl.when(j < mine_count)
+        def _():
+            y_send[c] = held.astype(BF16)
+            y_copy(c).start()
+
+        return carry
+
+    lax.fori_loop(0, chunks, state_chunk, 0)
+
+    skips = jnp.sum(jnp.where(hr == hc, jnp.broadcast_to(skip_ref[...], (heads, heads)), 0.0), axis=1, keepdims=True)
+    skip_row[...] = jnp.broadcast_to(jnp.sum(ones * skips, axis=0, keepdims=True), (8, inner))
+    grows, turned = turned_pieces(grow), ld.T
+    for b in range(blocks):
+        sc = lax.dot_general(c_mat[b], b_mat[b], (((1,), (1,)), ((), ())), preferred_element_type=F32)
+        score[b] = jnp.where(r_id >= c_id, sc, 0.0)
+        t_exp[b] = grows[b]
+        for c in range(chunks):
+            at = b * heads + c * per
+            ld_row[b, c] = ld[at : at + per]
+            st_row[b, c] = step[at : at + per]
+            ld_col[b, c] = turned[:, at : at + per]
     dec_copy.wait_recv()
     is_odd = odd.astype(F32)
 
-    def serve(c):
+    def serve(m):
+        c = odd * mine_count + m
         lanes = pl.ds(pl.multiple_of(c * LANES, LANES), LANES)
         y_copy(c).wait_recv()
         own = final[:, lanes]
         other = y_recv[c].astype(F32)
         d_own = decay_own[0:1, lanes]
         d_other = decay_other[0:1, lanes]
+        y_send[c] = ((1.0 - is_odd) * own).astype(BF16)
         enter[:, lanes] = is_odd * other
 
         @pl.when(place < rows - 1)
@@ -247,7 +262,17 @@
 
         @pl.when(place > 0)
         def _():
-            enter[:, lanes] += z_recv[c].astype(F32) * (1.0 - is_odd + is_odd * d_other)
+            before = z_recv[c].astype(F32)
+            enter[:, lanes] += before * (1.0 - is_odd + is_odd * d_other)
+            y_send[c] = ((1.0 - is_odd) * own + before * (is_odd + (1.0 - is_odd) * d_own)).astype(BF16)
+
+        y_copy(c).start()
+
+    def accept(m, carry):
+        c = (1 - odd) * mine_count + m
+        y_copy(c).wait_recv()
+        enter[:, pl.ds(pl.multiple_of(c * LANES, LANES), LANES)] = y_recv[c].astype(F32)
+        return carry
 
     first_head = lax.broadcasted_iota(jnp.int32, (1, 2 * width), 1) < width
     left = jnp.where(first_head, 1.0, 0.0).astype(BF16)
@@ -273,23 +298,20 @@
                 )
 
     def slot(j, carry):
-        c = j - 2 - 2 * place
-
-        @pl.when((c >= 0) & (c < chunks))
-        def _():
-            serve(c)
+        m = j - 2 * place
+
+        @pl.when((m >= 0) & (m < mine_count))
+        def _():
+            serve(m)
 
         @pl.when(j < chunks)
         def _():
-            state_chunk(j)
-
-        @pl.when((j >= chunks) & (j < 2 * chunks))
-        def _():
-            intra(j - chunks)
-
-        return carry
-
-    lax.fori_loop(0, max(2 * chunks, chunks + 2 * rows), slot, 0)
+            intra(j)
+
+        return carry
+
+    lax.fori_loop(0, max(chunks, mine_count + 2 * (rows - 1)), slot, 0)
+    lax.fori_loop(0, mine_count, accept, 0)
     for load in loads[7:]:
         load.wait()
     fetch_all(lambda copy: copy.wait())
@@ -309,7 +331,7 @@
         scale = lax.rsqrt(power * (1.0 / inner) + 1e-05)
         for c in range(chunks):
             lanes = pl.ds(c * LANES, LANES)
-            n_buf[token, lanes] = (y_ref[token, lanes] * scale * gain_ref[:, lanes]).astype(BF16)
+            x_ref[token, lanes] = (y_ref[token, lanes] * scale * gain_ref[:, lanes]).astype(BF16)
 
     def near_copy(src, dst, s, r, i):
         return send(src.at[i], dst.at[i], s.at[i], r.at[i], {"head": near})
@@ -323,13 +345,13 @@
 
         def pair_piece(c, carry):
             i = part * pieces + c
-            s1[i] = jnp.dot(n_buf[token, :], w_buf[c], preferred_element_type=F32).astype(BF16)
+            s1[i] = jnp.dot(x_ref[token, :], w_buf[c], preferred_element_type=F32).astype(BF16)
             near_copy(s1, r1, s1s, s1r, i).start()
             return carry
 
         def far_piece(c, carry):
             i = part * pieces + c
-            summed = jnp.dot(n_buf[token, :], w_buf[pieces + c], preferred_element_type=F32)
+            summed = jnp.dot(x_ref[token, :], w_buf[pieces + c], preferred_element_type=F32)
             near_copy(s1, r1, s1s, s1r, i).wait_recv()
             s2[i] = (summed + r1[i].astype(F32)).astype(BF16)
             far_copy(i).start()
@@ -340,9 +362,9 @@
         return carry
 
     def second(c, carry):
-        s3[c] = jnp.dot(n_buf[...], w_buf[2 * pieces + c], preferred_element_type=F32).astype(BF16)
+        s3[c] = jnp.dot(x_ref[...], w_buf[2 * pieces + c], preferred_element_type=F32).astype(BF16)
         near_copy(s3, r3, s3s, s3r, c).start()
-        keep[c] = jnp.dot(n_buf[...], w_buf[3 * pieces + c], preferred_element_type=F32)
+        keep[c] = jnp.dot(x_ref[...], w_buf[3 * pieces + c], preferred_element_type=F32)
         return carry
 
     def third(c, carry):
@@ -376,10 +398,12 @@
 
     def drain_state(c, carry):
         y_copy(c).wait_send()
-
+        return carry
+
+    def drain_chain(m, carry):
         @pl.when(place < rows - 1)
         def _():
-            z_copy(c).wait_send()
+            z_copy(odd * mine_count + m).wait_send()
 
         return carry
 
@@ -393,6 +417,7 @@
         return carry
 
     lax.fori_loop(0, chunks, drain_state, 0)
+    lax.fori_loop(0, mine_count, drain_chain, 0)
     lax.fori_loop(0, blocks * pieces, drain_first, 0)
     lax.fori_loop(0, pieces, drain_second, 0)
 
@@ -437,6 +462,7 @@
             vmem((tokens, inner), BF16),
             vmem((blocks, state, SPAN), BF16),
             vmem((blocks, SPAN, state), BF16),
+            vmem((blocks, SPAN, state), BF16),
             vmem((blocks, SPAN, SPAN), F32),
             vmem((blocks, chunks, per, SPAN), F32),
             vmem((blocks, chunks, per, SPAN), F32),
@@ -457,7 +483,6 @@
             moved,
             moved,
             moved,
-            vmem((tokens, inner), BF16),
             parts,
             parts,
             parts,

time: 65.8 us -> 58.2 us (0.88)
  Pallas kernels: 63.4 us -> 55.8 us
    pallas_call x1, Pallas kernels: 63.4 us -> 55.8 us  [on_device(): pl.pallas_call(functools.partial(layer_kernel, n_seq), name='layer', out_...]
where the time goes in v4:
time: 58.2 us; the launch traced here: 58 us
  Pallas kernels  55.8 us (96%)
  local copies, waits for them, and re-layouts  2.26 us (4%)
    pallas_call x1, Pallas kernels, on_device(): pl.pallas_call(functools.partial(layer_kernel, n_seq), name='layer', out_...  55.8 us
    unnamed x1, local copies, waits for them, and re-layouts  2.26 us

profile of v4, /device:TPU:24, one launch (start us, length us, event | category | flops | bytes accessed | tf_op | source)
XLA Modules:
  0.0 58.0 jit_solution(11100701863683835223)
XLA Ops:
  0.0 55.8 %layer.1 = bf16[1024,512]{1,0:T(8,128)(2,1)} custom-call(bf16[512,2048]{1,0:T(8,128)(2,1)} %x_hbm.1, bf16[512,256]{1,0:T(8,128)(2,1)} %bitcast.5, bf16[512,2048]{1,0:T(8,128)(2,1)} %z_hbm.1, bf16[32,512]{1,0:T(8,128)(2,1)} %dt_hbm.1, f32[1,32]{1,0:T(1,128)} %bitcast.8, f32[4,2048]{1,0:T(4,128)} %cx_hbm.1, f32[1,1024]{1,0:T(1,128)} %bitcast.7, ...), custom_call_target="tpu_custom_call" | custom-call | tf_op jit(solution)/shard_map/layer/pallas_call | solution.py:443
  55.8 2.3 %copy.12 = bf16[1024,512]{1,0:T(8,128)(2,1)} copy(bf16[1024,512]{1,0:T(8,128)(2,1)} %layer.1) | data formatting | bytes 2097152
